TPU v7x, 32 devices: a whole 2x2x4 slice. The times are simulated.
32 devices in a mesh: seq: 8 (over y, x, core), tp: 4 (over z).
Axes of the slice: x: 2, y: 2, z: 4, core: 2. Of those that a mesh axis runs over, the one named last changes fastest.
Arguments:
- tokens: bfloat16 [7168, 8192], P('seq', 'tp'), may hold values from -500 to 500
- query_tokens: bfloat16 [512, 8192], P('seq', 'tp'), may hold values from -500 to 500
- norm_gain: float32 [8192], replicated, may hold values from 0.1 to 1.9
- w_query: bfloat16 [8192, 4096], P(None, 'tp'), may hold values from -0.125 to 0.125
- w_key: bfloat16 [8192, 512], P('seq', 'tp'), may hold values from -0.0625 to 0.0625
- w_value: bfloat16 [8192, 512], P('seq', 'tp'), may hold values from -0.25 to 0.25
- cache_key: bfloat16 [1536, 512], P('seq', 'tp'), may hold values from -122 to 122
- cache_value: bfloat16 [1536, 512], P('seq', 'tp'), may hold values from -24 to 24
- seg_lengths: int32 [56], replicated, may hold values from 0 to 128, as said below
- prompt_query: int32 [56], replicated, may hold values from 0 to 7
- query_lengths: int32 [8], replicated, may hold values from 16 to 64
- assignment: int32 [56], replicated, may hold values from -1 to 31, as said below
Outputs:
- block_out: bfloat16 [4096, 4096], P('seq', 'tp')
- query_out: bfloat16 [512, 4096], P('seq', 'tp')
Inputs may be any that keep to these rules, and one draw needn't show every extreme that they name: `seg_lengths`: A slot without a passage has length 0, a live one 128 // 3 to 128. The live slots of a device come first. A device and the device half the seq axis away hold 8 live slots together, one of them 4 or more; some device holds 7. `assignment`: -1 exactly for the slots of length 0; the live slots carry the prompt positions 0 to 31, each once, and position p belongs to device p // 4. A live slot's position belongs to its own device or to the device half the seq axis away; every device gives at least one and at most 4 positions of that other device, and in every draw some device gives 4.
All inputs are finite; a program needn't handle non-finite values.
Results may differ from a plain program's by a relative error of at most 0.014.
The roundings to bfloat16 on the way count: a program that leaves them out, or rounds other values in their place, can miss the bound.
Values may be sent and summed in bfloat16 or wider, within the bound.
A program may use at most 128 MiB of HBM per device.

v0:
```python
import math

import jax
import jax.numpy as jnp
from jax import lax
from jax.sharding import PartitionSpec as P

HEAD_DIM = 128
BLK = 128
INSTR = 1536
QLEN = 64
BAL = 4
SLOTS = 7


eps_norm = 1e-05
rope_base = 500000.0
masked_score = -1e30


def passed_along(block, axis, distance):
    devices = range(lax.axis_size(axis))
    route = [((i - distance) % len(devices), i) for i in devices]
    return lax.ppermute(block, axis, route)


def normalize(row_block, norm_gain):
    values = row_block.astype(jnp.float32)
    mean_square = jnp.mean(values * values, axis=-1, keepdims=True)
    return (values * lax.rsqrt(mean_square + eps_norm) * norm_gain).astype(jnp.bfloat16)


def rotate(values, positions):
    half_width = values.shape[-1] // 2
    exponent = jnp.arange(half_width, dtype=jnp.float32) * (2.0 / values.shape[-1])
    inverse = jnp.power(jnp.float32(rope_base), -exponent)
    angle = positions.astype(jnp.float32)[:, None] * inverse[None, :]
    cosine = jnp.cos(angle)[:, None, :]
    sine_part = jnp.sin(angle)[:, None, :]
    first_half = values[..., :half_width]
    second_half = values[..., half_width:]
    return jnp.concatenate(
        [
            first_half * cosine - second_half * sine_part,
            second_half * cosine + first_half * sine_part,
        ],
        axis=-1,
    )


def attend(queries, keys_all, values_all, visible, live_rows):
    score_scale = 1.0 / math.sqrt(queries.shape[-1])
    scores = (
        jnp.einsum("rhgd,khd->hgrk", queries, keys_all, preferred_element_type=jnp.float32)
        * score_scale
    )
    scores = jnp.where(visible[None, None], scores, masked_score)
    largest = jnp.max(scores, axis=-1, keepdims=True)
    powers = jnp.exp(scores - largest)
    weights = (powers / jnp.sum(powers, axis=-1, keepdims=True)).astype(jnp.bfloat16)
    mixed = jnp.einsum("hgrk,khd->rhgd", weights, values_all, preferred_element_type=jnp.float32)
    mixed = jnp.where(live_rows[:, None, None, None], mixed, 0.0)
    return mixed.reshape(queries.shape[0], -1).astype(jnp.bfloat16)


def matmul(left, right):
    return jnp.dot(left, right, preferred_element_type=jnp.float32)


def body(
    tokens,
    query_tokens,
    norm_gain,
    w_query,
    w_key,
    w_value,
    cache_key,
    cache_value,
    seg_lengths,
    prompt_query,
    query_lengths,
    assignment,
):
    seq_count = lax.axis_size("seq")
    device = lax.axis_index("seq")
    local_cols = tokens.shape[1]
    kv_local = w_key.shape[1] // HEAD_DIM
    heads_local = w_query.shape[1] // HEAD_DIM
    group_size = heads_local // kv_local
    local_queries = query_tokens.shape[0] // QLEN
    half_axis = seq_count // 2
    extra_count = BAL
    partner = (device + half_axis) % seq_count
    block_ids = jnp.arange(BAL, dtype=jnp.int32)
    extra_ids = jnp.arange(extra_count, dtype=jnp.int32)

    def slot_routes(owner):
        plan = lax.dynamic_slice_in_dim(assignment, owner * SLOTS, SLOTS)
        target = jnp.where(plan >= 0, plan // BAL, -1)
        spot = jnp.where(plan >= 0, plan % BAL, -1)
        return (target, spot)

    my_target, my_spot = slot_routes(device)
    far_target, far_spot = slot_routes(partner)
    leaving = my_target == partner
    leave_rank = jnp.cumsum(leaving.astype(jnp.int32)) - 1
    arriving = far_target == device
    arrive_rank = jnp.cumsum(arriving.astype(jnp.int32)) - 1
    send_hot = (leaving[None, :] & (leave_rank[None, :] == extra_ids[:, None])).astype(jnp.bfloat16)
    keep_hot = ((my_target == device)[None, :] & (my_spot[None, :] == block_ids[:, None])).astype(
        jnp.bfloat16
    )
    take_hot = jnp.any(
        arriving[None, None, :]
        & (arrive_rank[None, None, :] == extra_ids[None, :, None])
        & (far_spot[None, None, :] == block_ids[:, None, None]),
        axis=2,
    ).astype(jnp.bfloat16)
    flat = tokens.reshape(SLOTS, -1)
    incoming_rows = passed_along(
        matmul(send_hot, flat).astype(jnp.bfloat16).reshape(extra_count, BLK, -1), "seq", half_axis
    )
    placed = matmul(keep_hot, tokens.reshape(SLOTS, -1)) + matmul(
        take_hot, incoming_rows.reshape(extra_count, -1)
    )
    work_rows = placed.astype(jnp.bfloat16).reshape(BAL * BLK, local_cols)
    work_count = BAL
    here_match = assignment[None, :] == (device * BAL + block_ids)[:, None]
    lengths_here = jnp.sum(jnp.where(here_match, seg_lengths[None, :], 0), axis=1)
    owners_here = jnp.sum(jnp.where(here_match, prompt_query[None, :], 0), axis=1)
    passage_total = work_count * BLK
    query_table = jnp.arange(query_lengths.shape[0], dtype=jnp.int32)
    offsets_here = jnp.sum(
        jnp.where(owners_here[:, None] == query_table[None, :], query_lengths[None, :], 0), axis=1
    )
    my_lengths = lax.dynamic_slice_in_dim(query_lengths, device * local_queries, local_queries)
    query_cols = jnp.arange(QLEN, dtype=jnp.int32)
    text_positions = jnp.tile(INSTR + query_cols, local_queries)
    full_blocks, full_query = (
        lax.all_gather(work_rows, "tp", axis=1, tiled=True),
        lax.all_gather(query_tokens, "tp", axis=1, tiled=True),
    )
    normed = normalize(jnp.concatenate([full_blocks, full_query], axis=0), norm_gain)
    every_query = matmul(normed, w_query)
    every_keys = matmul(normed, lax.all_gather(w_key, "seq", axis=0, tiled=True))
    every_values = matmul(normed, lax.all_gather(w_value, "seq", axis=0, tiled=True))
    block_query = every_query[:passage_total]
    text_query = every_query[passage_total:]
    block_keys = every_keys[:passage_total]
    block_values = every_values[:passage_total]
    rotated = rotate(
        every_keys[passage_total:].reshape(local_queries * QLEN, kv_local, HEAD_DIM), text_positions
    )
    rotated = rotated.astype(jnp.bfloat16).reshape(local_queries * QLEN, kv_local * HEAD_DIM)
    rounded = every_values[passage_total:].astype(jnp.bfloat16)
    gathered = (
        lax.all_gather(rotated, "seq", axis=0, tiled=True),
        lax.all_gather(rounded, "seq", axis=0, tiled=True),
    )
    cached = (
        lax.all_gather(cache_key, "seq", axis=0, tiled=True),
        lax.all_gather(cache_value, "seq", axis=0, tiled=True),
    )
    prefix = (rotated, rounded, gathered, cached)
    own_keys, own_values, gathered, cached = prefix
    all_text_keys = gathered[0].reshape(-1, QLEN, kv_local, HEAD_DIM)
    all_text_values = gathered[1].reshape(-1, QLEN, kv_local, HEAD_DIM)
    cache_keys = cached[0].reshape(-1, kv_local, HEAD_DIM)
    cache_values = cached[1].reshape(-1, kv_local, HEAD_DIM)
    cache_rows = cache_keys.shape[0]
    passage_rows = jnp.arange(BLK, dtype=jnp.int32)
    passage_positions = (INSTR + offsets_here[:, None] + passage_rows[None, :]).reshape(-1)
    rotated_query = rotate(
        block_query.reshape(passage_total, heads_local, HEAD_DIM), passage_positions
    )
    rotated_query = rotated_query.astype(jnp.bfloat16).reshape(
        work_count, BLK, kv_local, group_size, HEAD_DIM
    )
    rotated_keys = rotate(block_keys.reshape(passage_total, kv_local, HEAD_DIM), passage_positions)
    rotated_keys = rotated_keys.astype(jnp.bfloat16).reshape(work_count, BLK, kv_local, HEAD_DIM)
    rounded_values = block_values.astype(jnp.bfloat16).reshape(work_count, BLK, kv_local, HEAD_DIM)
    passage_causal = passage_rows[None, :] <= passage_rows[:, None]

    def block_step(inputs):
        queries, passage_keys, passage_values, owner_query, offset, length = inputs
        prompt_keys = jnp.concatenate(
            [
                cache_keys,
                lax.dynamic_index_in_dim(all_text_keys, owner_query, 0, keepdims=False),
                passage_keys,
            ],
            axis=0,
        )
        prompt_values = jnp.concatenate(
            [
                cache_values,
                lax.dynamic_index_in_dim(all_text_values, owner_query, 0, keepdims=False),
                passage_values,
            ],
            axis=0,
        )
        visible = jnp.concatenate(
            [
                jnp.ones((BLK, cache_rows), dtype=bool),
                jnp.broadcast_to(query_cols[None, :] < offset, (BLK, QLEN)),
                passage_causal,
            ],
            axis=1,
        )
        return attend(queries, prompt_keys, prompt_values, visible, passage_rows < length)

    block_out = lax.map(
        block_step,
        (rotated_query, rotated_keys, rounded_values, owners_here, offsets_here, lengths_here),
    )
    out_cols = heads_local * HEAD_DIM
    block_out = block_out.reshape(passage_total, out_cols)
    text_rotated = rotate(
        text_query.reshape(local_queries * QLEN, heads_local, HEAD_DIM), text_positions
    )
    text_rotated = text_rotated.astype(jnp.bfloat16).reshape(
        local_queries, QLEN, kv_local, group_size, HEAD_DIM
    )
    own_key_table = own_keys.reshape(local_queries, QLEN, kv_local, HEAD_DIM)
    own_value_table = own_values.reshape(local_queries, QLEN, kv_local, HEAD_DIM)

    def query_step(inputs):
        queries, text_keys, text_values, length = inputs
        keys_all = jnp.concatenate([cache_keys, text_keys], axis=0)
        values_all = jnp.concatenate([cache_values, text_values], axis=0)
        causal = (query_cols[None, :] <= query_cols[:, None]) & (query_cols[None, :] < length)
        visible = jnp.concatenate([jnp.ones((QLEN, cache_rows), dtype=bool), causal], axis=1)
        return attend(queries, keys_all, values_all, visible, query_cols < length)

    query_out = lax.map(query_step, (text_rotated, own_key_table, own_value_table, my_lengths))
    query_out = query_out.reshape(local_queries * QLEN, heads_local * HEAD_DIM)
    return (block_out, query_out)


def solution(mesh):
    placed = (
        P("seq", "tp"),
        P("seq", "tp"),
        P(),
        P(None, "tp"),
        P("seq", "tp"),
        P("seq", "tp"),
        P("seq", "tp"),
        P("seq", "tp"),
        P(),
        P(),
        P(),
        P(),
    )
    return jax.shard_map(
        body,
        mesh=mesh,
        in_specs=placed,
        out_specs=(P("seq", "tp"), P("seq", "tp")),
        check_vma=False,
    )
```

profile of v0, /device:TPU:0, one launch (start us, length us, event | category | flops | bytes accessed | tf_op | source)
XLA Modules:
  0.0 376.3 jit_solution(8774435257396988127)
XLA Ops:
  7.2 0.8 convert_bitcast_fusion.2
  8.2 9.7 %reshape.619 = bf16[7,262144]{1,0:T(8,128)(2,1)} reshape(bf16[896,2048]{1,0:T(8,128)(2,1)} %param.14) | data formatting | bytes 7340032 | tf_op jit(solution)/shard_map/reshape | solution.py:123
  18.0 3.4 convolution_convert_fusion
  21.4 1.2 copy.61
  22.6 3.0 collective-permute-start
  26.3 3.4 fusion.83
  29.7 41.6 %collective-permute-done = bf16[4,128,2048]{2,1,0:T(8,128)(2,1)} collective-permute-done((bf16[4,128,2048]{2,1,0:T(8,128)(2,1)S(1)}, bf16[4,128,2048]{2,1,0:T(8,128)(2,1)}, u32[]{:S(2)}, u32[]{:S(2)}) %collective-permute-start) | collective-permute-done | bytes 2097184 | tf_op jit(solution)/shard_map/ppermute | solution.py:24
  71.3 3.2 copy.52
  74.6 1.4 fusion.35
  76.0 3.3 reshape.624
  79.3 0.7 all-gather.11.cloned.1.call-update
  82.0 9.8 %all_gather.31 = bf16[1536,128]{1,0:T(8,128)(2,1)S(1)} all-gather(bf16[192,128]{1,0:T(8,128)(2,1)S(1)} %copy-done.9), channel_id=1, replica_groups=mesh['seq'=8,'tp'=4] {'seq'}, dimensions={0}, use_global_device_ids=true | all-gather | bytes 442368 | tf_op jit(solution)/shard_map/all_gather | solution.py:161
  91.8 10.5 %all_gather.28 = bf16[1536,128]{1,0:T(8,128)(2,1)} all-gather(bf16[192,128]{1,0:T(8,128)(2,1)S(1)} %copy-done.10), channel_id=1, replica_groups=mesh['seq'=8,'tp'=4] {'seq'}, dimensions={0}, use_global_device_ids=true | all-gather | bytes 442368 | tf_op jit(solution)/shard_map/all_gather | solution.py:162
  102.3 0.7 fusion.81
  104.1 0.7 concatenate.93
  104.7 125.9 %all-gather.5.cloned.1.call-done = bf16[512,8192]{1,0:T(8,128)(2,1)} async-done(((bf16[512,2048]{1,0:T(8,128)(2,1)}), bf16[512,8192]{1,0:T(8,128)(2,1)}) %all-gather.5.cloned.1.call-update) | async-done | bytes 8388624 | tf_op jit(solution)/shard_map/all_gather | solution.py:140
  230.6 5.7 %fusion.36 = f32[576]{0:T(1024)S(1)} fusion(bf16[64,8192]{1,0:T(8,128)(2,1)} %all-gather.7.cloned.1.call-done, bf16[512,8192]{1,0:T(8,128)(2,1)} %all-gather.5.cloned.1.call-done), kind=kLoop, calls=%fused_computation.46 | loop fusion | flops 28310976 | bytes 9439488 | tf_op jit(solution)/shard_map/reduce_sum | solution.py:29
  236.3 6.4 %fusion.38 = bf16[576,8192]{1,0:T(8,128)(2,1)S(1)} fusion(f32[8192]{0:T(1024)S(1)} %copy-done.11, f32[576]{0:T(1024)S(1)} %add_rsqrt_fusion, bf16[64,8192]{1,0:T(8,128)(2,1)S(1)} %copy-done.2, bf16[512,8192]{1,0:T(8,128)(2,1)} %all-gather.5.cloned.1.call-done), kind=kLoop, calls=%fused_computation.48 | loop fusion | flops 33030144 | bytes 18909440 | tf_op jit(solution)/shard_map/convert_element_type | solution.py:30
  242.7 16.3 %fusion.99 = f32[576,1024]{1,0:T(8,128)S(1)} fusion(bf16[576,8192]{1,0:T(8,128)(2,1)S(1)} %fusion.38, bf16[8192,1024]{1,0:T(8,128)(2,1)} %param.17), kind=kOutput, calls=%fused_computation.163 | convolution fusion | flops 9663676416 | bytes 28573696 | tf_op jit(solution)/shard_map/dot_general | solution.py:67
  259.0 6.6 %fusion.98 = f32[576,128]{1,0:T(8,128)S(1)} fusion(bf16[576,8192]{1,0:T(8,128)(2,1)} %copy-done, bf16[8192,128]{1,0:T(8,128)(2,1)} %all-gather.11.cloned.1.call-done), kind=kOutput, calls=%fused_computation.162 | convolution fusion | flops 1207959552 | bytes 11829248 | tf_op jit(solution)/shard_map/dot_general | solution.py:67
  265.8 22.5 %all-gather.9.cloned.1.call-done = bf16[8192,128]{1,0:T(8,128)(2,1)} async-done(((bf16[1024,128]{1,0:T(8,128)(2,1)}), bf16[8192,128]{1,0:T(8,128)(2,1)}) %all-gather.9.cloned.1.call-update) | async-done | bytes 2097168 | tf_op jit(solution)/shard_map/all_gather | solution.py:146
  288.3 6.9 %convolution_convert_fusion.1 = bf16[576,128]{1,0:T(8,128)(2,1)S(1)} fusion(bf16[576,8192]{1,0:T(8,128)(2,1)} %copy-done, bf16[8192,128]{1,0:T(8,128)(2,1)} %all-gather.9.cloned.1.call-done), kind=kOutput, calls=%fused_computation.58 | convolution fusion | flops 1208033280 | bytes 11681792 | tf_op jit(solution)/shard_map/dot_general | solution.py:67
  295.8 0.9 fusion.97
  297.3 0.7 fusion.51
  298.1 0.7 copy.62
  298.9 1.8 copy.46
  300.7 1.9 subtract_convert_fusion
  303.0 0.7 pad_maximum_fusion.1
  303.7 0.8 copy.41
  304.5 1.2 fusion.65
  305.8 9.4 %all_gather.30 = bf16[512,128]{1,0:T(8,128)(2,1)S(1)} all-gather(bf16[64,128]{1,0:T(8,128)(2,1)S(1)} %pad_maximum_fusion.3), channel_id=1, replica_groups=mesh['seq'=8,'tp'=4] {'seq'}, dimensions={0}, use_global_device_ids=true | all-gather | bytes 147456 | tf_op jit(solution)/shard_map/all_gather | solution.py:157
  315.2 8.2 %all_gather.27 = bf16[512,128]{1,0:T(8,128)(2,1)S(1)} all-gather(bf16[64,128]{1,0:T(8,128)(2,1)S(1)} %get-tuple-element.217), channel_id=1, replica_groups=mesh['seq'=8,'tp'=4] {'seq'}, dimensions={0}, use_global_device_ids=true | all-gather | bytes 147456 | tf_op jit(solution)/shard_map/all_gather | solution.py:158
  323.6 45.7 %while.3 = (s32[]{:T(128)}, bf16[4,128,1024]{2,1,0:T(8,128)(2,1)}, s32[4]{0:T(128)S(1)}, s32[4]{0:T(128)S(1)}, bf16[8,64,1,128]{3,1,2,0:T(8,128)(2,1)S(1)}, /*in...) while((s32[]{:T(128)}, bf16[4,128,1024]{2,1,0:T(8,128)(2,1)}, ...), condition=%wide.region_10.11_spmd.clone, body=%wide.region_7.10_spmd.clone.sunk | while | flops 930357120 | bytes 24833520 | solution.py:212
  326.4 0.7 dynamic_slice.94
  327.1 0.7 iota_compare_fusion.14
  328.1 1.2 fusion.115
  329.3 1.5 fusion.116
  330.8 0.7 dynamic_slice.96
  331.5 0.7 iota_compare_fusion.15
  332.2 2.0 fusion.117
  334.3 0.7 constant_dynamic-update-slice_fusion.2
  337.8 0.7 dynamic_slice.94
  338.5 0.7 iota_compare_fusion.14
  339.6 1.2 fusion.115
  340.7 1.5 fusion.116
  342.2 0.7 dynamic_slice.96
  342.9 0.7 iota_compare_fusion.15
  343.6 2.0 fusion.117
  345.7 0.7 constant_dynamic-update-slice_fusion.2
  349.2 0.7 dynamic_slice.94
  349.9 0.7 iota_compare_fusion.14
  351.0 1.2 fusion.115
  352.1 1.5 fusion.116
  353.6 0.7 dynamic_slice.96
  354.3 0.7 iota_compare_fusion.15
  355.0 2.0 fusion.117
  357.2 0.7 constant_dynamic-update-slice_fusion.2
  360.6 0.7 dynamic_slice.94
  361.3 0.7 iota_compare_fusion.14
  362.4 1.2 fusion.115
  363.6 1.5 fusion.116
  365.7 0.7 iota_compare_fusion.15
  366.4 2.0 fusion.117
  368.6 0.7 constant_dynamic-update-slice_fusion.2
  (141 shorter events, 11.0 us)
Async XLA Ops:
  7.2 97.6 %all-gather.7.cloned.1.call-start = ((), (), s32[]{:S(2)}) async-start(), calls=%async_computation.1 | async-start | bytes 1310720 | tf_op jit(solution)/shard_map/all_gather | solution.py:141
  21.4 4.6 %copy-start.14 = (s32[56]{0:T(128)S(1)}, s32[56]{0:T(128)}, u32[]{:S(2)}) copy-start(s32[56]{0:T(128)} %param.25) | copy-start | bytes 676
  22.6 48.8 %collective-permute-start = (bf16[4,128,2048]{2,1,0:T(8,128)(2,1)S(1)}, bf16[4,128,2048]{2,1,0:T(8,128)(2,1)}, u32[]{:S(2)}, u32[]{:S(2)}) collective-permute-start(bf16[4,128,2048]{2,1,0:T(8,128)(2,1)S(1)} %bitcast.198), channel_id=1, source_target_pairs={{16,0},{20,4},{24,8},{28,12},{0,16},{4,20},{8,24},{12,28},{17,1},{... | collective-permute-start | bytes 6291464 | tf_op jit(solution)/shard_map/ppermute | solution.py:24
  25.6 205.0 %all-gather.5.cloned.1.call-start = ((), (), s32[]{:S(2)}) async-start(), calls=%async_computation | async-start | bytes 10485760 | tf_op jit(solution)/shard_map/all_gather | solution.py:140
  76.0 4.7 %copy-start.27 = (s32[8]{0:T(128)S(1)}, s32[8]{0:T(128)}, u32[]{:S(2)}) copy-start(s32[8]{0:T(128)} %param.24) | copy-start | bytes 100
  76.0 6.0 %copy-start.9 = (bf16[192,128]{1,0:T(8,128)(2,1)S(1)}, bf16[192,128]{1,0:T(8,128)(2,1)}, u32[]{:S(2)}) copy-start(bf16[192,128]{1,0:T(8,128)(2,1)} %param.20) | copy-start | bytes 147460
  76.0 15.8 %copy-start.10 = (bf16[192,128]{1,0:T(8,128)(2,1)S(1)}, bf16[192,128]{1,0:T(8,128)(2,1)}, u32[]{:S(2)}) copy-start(bf16[192,128]{1,0:T(8,128)(2,1)} %param.21) | copy-start | bytes 147460
  76.0 26.3 %copy-start.22 = (s32[56]{0:T(128)S(1)}, s32[56]{0:T(128)}, u32[]{:S(2)}) copy-start(s32[56]{0:T(128)} %param.23) | copy-start | bytes 676
  76.0 26.3 %copy-start.23 = (s32[56]{0:T(128)S(1)}, s32[56]{0:T(128)}, u32[]{:S(2)}) copy-start(s32[56]{0:T(128)} %param.22) | copy-start | bytes 676
  79.3 179.7 %all-gather.11.cloned.1.call-start = ((), (), s32[]{:S(2)}) async-start(), calls=%async_computation.3 | async-start | bytes 2359296 | tf_op jit(solution)/shard_map/all_gather | solution.py:145
  80.0 208.3 %all-gather.9.cloned.1.call-start = ((), (), s32[]{:S(2)}) async-start(), calls=%async_computation.2 | async-start | bytes 2359296 | tf_op jit(solution)/shard_map/all_gather | solution.py:146
  80.6 23.4 %copy-start.15 = (f32[64]{0:T(128)}, f32[64]{0:T(128)S(1)}, u32[]{:S(2)}) copy-start(f32[64]{0:T(128)S(1)} %negate_power_fusion) | copy-start | bytes 772
  80.6 23.4 %copy-start.18 = (f32[64]{0:T(128)}, f32[64]{0:T(128)S(1)}, u32[]{:S(2)}) copy-start(f32[64]{0:T(128)S(1)} %add_convert_fusion.2) | copy-start | bytes 772
  81.9 21.3 %copy-start.20 = (pred[64]{0:T(512)(128)(4,1)}, pred[64]{0:T(512)(128)(4,1)S(1)}, u32[]{:S(2)}) copy-start(pred[64]{0:T(512)(128)(4,1)S(1)} %iota_compare_fusion.9) | copy-start | bytes 196
  103.0 133.3 %copy-start.24 = (s32[4]{0:T(128)}, s32[4]{0:T(128)S(1)}, u32[]{:S(2)}) copy-start(s32[4]{0:T(128)S(1)} %get-tuple-element.321) | copy-start | bytes 52
  103.2 133.1 %copy-start.28 = (s32[4]{0:T(128)}, s32[4]{0:T(128)S(1)}, u32[]{:S(2)}) copy-start(s32[4]{0:T(128)S(1)} %select_reduce_fusion) | copy-start | bytes 52
  103.3 0.8 copy-start.12
  104.7 131.6 %copy-start.11 = (f32[8192]{0:T(1024)S(1)}, f32[8192]{0:T(1024)}, u32[]{:S(2)}) copy-start(f32[8192]{0:T(1024)} %param.16) | copy-start | bytes 98308
  104.7 131.6 %copy-start.2 = (bf16[64,8192]{1,0:T(8,128)(2,1)S(1)}, bf16[64,8192]{1,0:T(8,128)(2,1)}, u32[]{:S(2)}) copy-start(bf16[64,8192]{1,0:T(8,128)(2,1)} %all-gather.7.cloned.1.call-done) | copy-start | bytes 3145732
  242.7 16.3 %copy-start = (bf16[576,8192]{1,0:T(8,128)(2,1)}, bf16[576,8192]{1,0:T(8,128)(2,1)S(1)}, u32[]{:S(2)}) copy-start(bf16[576,8192]{1,0:T(8,128)(2,1)S(1)} %fusion.38) | copy-start | bytes 28311556
  259.0 6.7 %copy-start.1 = (f32[576,1024]{1,0:T(8,128)}, f32[576,1024]{1,0:T(8,128)S(1)}, u32[]{:S(2)}) copy-start(f32[576,1024]{1,0:T(8,128)S(1)} %fusion.99) | copy-start | bytes 7077892
  265.7 29.7 %copy-start.16 = (f32[64]{0:T(128)S(1)}, f32[64]{0:T(128)}, u32[]{:S(2)}) copy-start(f32[64]{0:T(128)} %copy-done.15) | copy-start | bytes 772
  265.7 29.7 %copy-start.19 = (f32[64]{0:T(128)S(1)}, f32[64]{0:T(128)}, u32[]{:S(2)}) copy-start(f32[64]{0:T(128)} %copy-done.18) | copy-start | bytes 772
  265.8 30.0 %copy-start.6 = (pred[64,1600]{1,0:T(8,128)(4,1)S(1)}, pred[64,1600]{1,0:T(8,128)(4,1)}, u32[]{:S(2)}) copy-start(pred[64,1600]{1,0:T(8,128)(4,1)} %concatenate.93) | copy-start | bytes 307204
  295.2 2.1 copy-start.3
  295.6 1.7 copy-start.7
  295.7 1.6 copy-start.4
  295.7 1.6 copy-start.21
  297.3 1.6 slice-start
  300.7 3.7 copy-start.13
  300.7 3.7 copy-start.17
  302.6 3.1 copy-start.8
  302.7 20.9 %slice-start.1 = ((bf16[576,128]{1,0:T(8,128)(2,1)}), bf16[512,128]{1,0:T(8,128)(2,1)S(1)}, s32[]{:S(2)}) async-start(bf16[576,128]{1,0:T(8,128)(2,1)} %copy-done.3), calls=%async_computation.5 | async-start | bytes 262144 | tf_op jit(solution)/shard_map/slice | solution.py:150
  302.7 20.9 %copy-start.5 = (bf16[1536,128]{1,0:T(8,128)(2,1)S(1)}, bf16[1536,128]{1,0:T(8,128)(2,1)}, u32[]{:S(2)}) copy-start(bf16[1536,128]{1,0:T(8,128)(2,1)} %all_gather.28) | copy-start | bytes 1179652
  302.7 20.9 %copy-start.25 = (s32[4]{0:T(128)S(1)}, s32[4]{0:T(128)}, u32[]{:S(2)}) copy-start(s32[4]{0:T(128)} %copy-done.24) | copy-start | bytes 52
  302.7 20.9 %copy-start.26 = (s32[4]{0:T(128)S(1)}, s32[4]{0:T(128)}, u32[]{:S(2)}) copy-start(s32[4]{0:T(128)} %get-tuple-element.320) | copy-start | bytes 52
  302.7 20.9 %copy-start.29 = (s32[4]{0:T(128)S(1)}, s32[4]{0:T(128)}, u32[]{:S(2)}) copy-start(s32[4]{0:T(128)} %copy-done.28) | copy-start | bytes 52
Sparse Core Ops, SparseCore 0:
  25.8 28.2 all-gather.6
  79.4 151.1 all-gather.4
  232.5 26.0 all-gather.10
  260.4 27.8 all-gather.8
where the time goes:
time: 383 us; the launch traced here: 376 us
  waiting for transfers between devices  191 us (50%)
  matrix products  52.4 us (14%)
  blocking collectives  38 us (10%)
  local copies, waits for them, and re-layouts  34.3 us (9%)
  other arithmetic  33.3 us (9%)
  between operations  14.9 us (4%)
  loops' own time  8.64 us (2%)
    all_gather x1, waiting for transfers between devices, body(): lax.all_gather(work_rows, 'tp', axis=1, tiled=True)  126 us
    ppermute x1, waiting for transfers between devices, passed_along(): return lax.ppermute(block, axis, route)  41.6 us
    dot_general x6, matrix products, matmul(): return jnp.dot(left, right, preferred_element_type=jnp.float32)  38 us
    all_gather x1, waiting for transfers between devices, body(): lax.all_gather(w_value, 'seq', axis=0, tiled=True)  22.5 us
    all_gather x1, blocking collectives, body(): lax.all_gather(cache_value, 'seq', axis=0, tiled=True)  10.5 us
    all_gather x1, blocking collectives, body(): lax.all_gather(cache_key, 'seq', axis=0, tiled=True)  9.81 us
    reshape x1, local copies, waits for them, and re-layouts, body(): tokens.reshape(SLOTS, -1)  9.74 us
    all_gather x1, blocking collectives, body(): lax.all_gather(rotated, 'seq', axis=0, tiled=True)  9.43 us
  transfers between devices with their start and end apart: 5, of which 3 were waited for; matrix products, arithmetic and copies ran while one was open for 13% of the time, Pallas kernels for 0%

commit v1 on v0

v1 whole, which is shorter than its diff:
```python
import math

import jax
import jax.numpy as jnp
from jax import lax
from jax.sharding import PartitionSpec as P

HEAD_DIM = 128
BLK = 128
INSTR = 1536
QLEN = 64
BAL = 4


eps_norm = 1e-05
rope_base = 500000.0
masked_score = -1e30


def passed_along(block, axis, distance):
    devices = range(lax.axis_size(axis))
    route = [((i - distance) % len(devices), i) for i in devices]
    return lax.ppermute(block, axis, route)


def rotate(values, positions):
    half_width = values.shape[-1] // 2
    exponent = jnp.arange(half_width, dtype=jnp.float32) * (2.0 / values.shape[-1])
    inverse = jnp.power(jnp.float32(rope_base), -exponent)
    angle = positions.astype(jnp.float32)[:, None] * inverse[None, :]
    cosine = jnp.cos(angle)[:, None, :]
    sine_part = jnp.sin(angle)[:, None, :]
    first_half = values[..., :half_width]
    second_half = values[..., half_width:]
    return jnp.concatenate(
        [
            first_half * cosine - second_half * sine_part,
            second_half * cosine + first_half * sine_part,
        ],
        axis=-1,
    )


def attend(queries, keys_all, values_all, visible, live_rows):
    score_scale = 1.0 / math.sqrt(queries.shape[-1])
    scores = (
        jnp.einsum("rhgd,khd->hgrk", queries, keys_all, preferred_element_type=jnp.float32)
        * score_scale
    )
    scores = jnp.where(visible[None, None], scores, masked_score)
    largest = jnp.max(scores, axis=-1, keepdims=True)
    powers = jnp.exp(scores - largest)
    weights = (powers / jnp.sum(powers, axis=-1, keepdims=True)).astype(jnp.bfloat16)
    mixed = jnp.einsum("hgrk,khd->rhgd", weights, values_all, preferred_element_type=jnp.float32)
    mixed = jnp.where(live_rows[:, None, None, None], mixed, 0.0)
    return mixed.reshape(queries.shape[0], -1).astype(jnp.bfloat16)


def matmul(left, right):
    return jnp.dot(left, right, preferred_element_type=jnp.float32)


def gather_rows(block, axis):
    count = lax.axis_size(axis)
    if count & (count - 1):
        return lax.all_gather(block, axis, axis=0, tiled=False)
    index = lax.axis_index(axis)
    held = block[None]
    bit = count // 2
    while bit:
        route = [(i, i ^ bit) for i in range(count)]
        other = lax.ppermute(held, axis, route)
        high = (index & bit) != 0
        held = jnp.stack([jnp.where(high, other, held), jnp.where(high, held, other)], axis=1)
        held = held.reshape((-1,) + block.shape)
        bit //= 2
    return held


def after(value, earlier):
    return lax.optimization_barrier((value, earlier))


def body(
    tokens,
    query_tokens,
    norm_gain,
    w_query,
    w_key,
    w_value,
    cache_key,
    cache_value,
    seg_lengths,
    prompt_query,
    query_lengths,
    assignment,
):
    seq_count = lax.axis_size("seq")
    device = lax.axis_index("seq")
    kv_local = w_key.shape[1] // HEAD_DIM
    heads_local = w_query.shape[1] // HEAD_DIM
    group_size = heads_local // kv_local
    local_queries = query_tokens.shape[0] // QLEN
    half_axis = seq_count // 2
    partner = (device + half_axis) % seq_count
    slots = tokens.shape[0] // BLK
    slot_ids = jnp.arange(assignment.shape[0], dtype=jnp.int32)
    my_lengths = lax.dynamic_slice_in_dim(query_lengths, device * local_queries, local_queries)
    query_cols = jnp.arange(QLEN, dtype=jnp.int32)
    passage_rows = jnp.arange(BLK, dtype=jnp.int32)

    def of_position(position, table):
        return jnp.sum(jnp.where(assignment == position, table, 0))

    def local_block(position):
        slot = of_position(position, slot_ids) - device * slots
        mine = (slot >= 0) & (slot < slots)
        start = jnp.clip(slot, 0, slots - 1) * BLK
        return mine, lax.dynamic_slice_in_dim(tokens, start, BLK, axis=0)

    def all_features(rows):
        gathered = lax.all_gather(rows, "tp", axis=0, tiled=False)
        values = gathered.astype(jnp.float32)
        gains = norm_gain.reshape(gathered.shape[0], 1, -1)
        mean_square = jnp.mean(values * values, axis=(0, 2), keepdims=True)
        normed = (values * lax.rsqrt(mean_square + eps_norm) * gains).astype(jnp.bfloat16)
        return normed.transpose(1, 0, 2).reshape(rows.shape[0], -1)

    full_query = all_features(query_tokens)

    packed = jnp.concatenate([w_key, w_value, cache_key, cache_value], axis=0)
    incoming = []
    shared = None
    for c in range(BAL):
        block = local_block(partner * BAL + c)[1]
        if c == 1:
            packed, incoming[0] = after(packed, incoming[0])
            shared = gather_rows(packed, "seq")
        if c:
            block, incoming[-1] = after(block, incoming[-1])
        incoming.append(passed_along(block, "seq", half_axis))
    blocks = []
    for c in range(BAL):
        mine, kept = local_block(device * BAL + c)
        blocks.append(jnp.where(mine, kept, incoming[c]))

    depth, cache_depth = w_key.shape[0], cache_key.shape[0]
    width = w_key.shape[1]
    w_both = jnp.concatenate([shared[:, :depth], shared[:, depth : 2 * depth]], axis=2)
    w_both = w_both.reshape(-1, 2 * width)
    cache_keys = shared[:, 2 * depth : 2 * depth + cache_depth].reshape(-1, kv_local, HEAD_DIM)
    cache_values = shared[:, 2 * depth + cache_depth :].reshape(-1, kv_local, HEAD_DIM)
    cache_rows = cache_keys.shape[0]

    def project(normed, positions):
        rows = normed.shape[0]
        queries = matmul(normed, w_query).reshape(rows, heads_local, HEAD_DIM)
        both = matmul(normed, w_both)
        queries = rotate(queries, positions).astype(jnp.bfloat16)
        keys = rotate(both[:, :width].reshape(rows, kv_local, HEAD_DIM), positions)
        values = both[:, width:].reshape(rows, kv_local, HEAD_DIM)
        return (
            queries.reshape(rows, kv_local, group_size, HEAD_DIM),
            keys.astype(jnp.bfloat16),
            values.astype(jnp.bfloat16),
        )

    text_positions = jnp.tile(INSTR + query_cols, local_queries)
    text_q, text_k, text_v = project(full_query, text_positions)
    text_all = gather_rows(jnp.stack([text_k, text_v]), "seq")
    text_all = text_all.reshape(seq_count, 2, local_queries, QLEN, kv_local, HEAD_DIM)

    query_out = []
    for n in range(local_queries):
        rows = slice(n * QLEN, (n + 1) * QLEN)
        keys_all = jnp.concatenate([cache_keys, text_k[rows]], axis=0)
        values_all = jnp.concatenate([cache_values, text_v[rows]], axis=0)
        length = my_lengths[n]
        causal = (query_cols[None, :] <= query_cols[:, None]) & (query_cols[None, :] < length)
        visible = jnp.concatenate([jnp.ones((QLEN, cache_rows), dtype=bool), causal], axis=1)
        query_out.append(attend(text_q[rows], keys_all, values_all, visible, query_cols < length))
    query_out = jnp.concatenate(query_out, axis=0)

    passage_causal = passage_rows[None, :] <= passage_rows[:, None]
    block_out = []
    for c in range(BAL):
        position = device * BAL + c
        length = of_position(position, seg_lengths)
        owner = of_position(position, prompt_query)
        offset = lax.dynamic_index_in_dim(query_lengths, owner, 0, keepdims=False)
        queries, keys, values = project(all_features(blocks[c]), INSTR + offset + passage_rows)
        text = lax.dynamic_slice(
            text_all,
            (owner // local_queries, 0, owner % local_queries, 0, 0, 0),
            (1, 2, 1) + text_all.shape[3:],
        )[0, :, 0]
        visible = jnp.concatenate(
            [
                jnp.ones((BLK, cache_rows), dtype=bool),
                jnp.broadcast_to(query_cols[None, :] < offset, (BLK, QLEN)),
                passage_causal,
            ],
            axis=1,
        )
        block_out.append(
            attend(
                queries,
                jnp.concatenate([cache_keys, text[0], keys], axis=0),
                jnp.concatenate([cache_values, text[1], values], axis=0),
                visible,
                passage_rows < length,
            )
        )
    return (jnp.concatenate(block_out, axis=0), query_out)


def solution(mesh):
    placed = (
        P("seq", "tp"),
        P("seq", "tp"),
        P(),
        P(None, "tp"),
        P("seq", "tp"),
        P("seq", "tp"),
        P("seq", "tp"),
        P("seq", "tp"),
        P(),
        P(),
        P(),
        P(),
    )
    return jax.shard_map(
        body,
        mesh=mesh,
        in_specs=placed,
        out_specs=(P("seq", "tp"), P("seq", "tp")),
        check_vma=False,
    )
```

time: 383 us -> 370 us (0.966)
  waiting for transfers between devices: 191 us -> 141 us
  local copies, waits for them, and re-layouts: 34.3 us -> 73.1 us
  blocking collectives: 38 us -> 0 us
  other arithmetic: 33.3 us -> 51.6 us
  between operations: 14.9 us -> 30.8 us
  starting transfers between devices: 3.36 us -> 14.1 us
  loops' own time: 8.64 us -> 0 us
    all_gather x4 -> x5, waiting for transfers between devices: 148 us -> 86.3 us  [all_features(): gathered = lax.all_gather(rows, 'tp', axis=0, tiled=False)]
    all_gather x4 -> x0, blocking collectives: 38 us -> none  [the longest x1 10.5 us: body(): lax.all_gather(cache_value, 'seq', axis=0, tiled=True)]
    dot_general x0 -> x1, local copies, waits for them, and re-layouts: none -> 21.1 us  [matmul(): return jnp.dot(left, right, preferred_element_type=jnp.float32)]
    transpose x0 -> x5, local copies, waits for them, and re-layouts: none -> 15.4 us  [all_features(): return normed.transpose(1, 0, 2).reshape(rows.shape[0], -1)]
    ppermute x0 -> x6, waiting for transfers between devices: none -> 14.8 us  [gather_rows(): other = lax.ppermute(held, axis, route)]
    transpose x0 -> x2, other arithmetic: none -> 9.38 us  [all_features(): return normed.transpose(1, 0, 2).reshape(rows.shape[0], -1)]
    another operation x1 -> x0, loops' own time: 8.64 us -> none  [body(): lax.map(block_step, (rotated_query, rotated_keys, rounded_values, owners_...]
    reshape x5 -> x11, local copies, waits for them, and re-layouts: 14.9 us -> 21.4 us  [the longest x10 21.4 us: all_features(): return normed.transpose(1, 0, 2).reshape(rows.shape[0], -1)]
  transfers between devices with their start and end apart: 5 -> 15, of which waited for: 3 -> 9; matrix products, arithmetic and copies ran while one was open for 13% -> 20% of each run, Pallas kernels for 0% -> 0%
where the time goes in v1:
time: 370 us; the launch traced here: 364 us
  waiting for transfers between devices  141 us (38%)
  local copies, waits for them, and re-layouts  73.1 us (20%)
  matrix products  53.3 us (14%)
  other arithmetic  51.6 us (14%)
  between operations  30.8 us (8%)
  starting transfers between devices  14.1 us (4%)
    all_gather x5, waiting for transfers between devices, all_features(): gathered = lax.all_gather(rows, 'tp', axis=0, tiled=False)  86.3 us
    ppermute x4, waiting for transfers between devices, passed_along(): return lax.ppermute(block, axis, route)  40 us
    dot_general x10, matrix products, matmul(): return jnp.dot(left, right, preferred_element_type=jnp.float32)  38.1 us
    reshape x10, local copies, waits for them, and re-layouts, all_features(): return normed.transpose(1, 0, 2).reshape(rows.shape[0], -1)  21.4 us
    dot_general x1, local copies, waits for them, and re-layouts, matmul(): return jnp.dot(left, right, preferred_element_type=jnp.float32)  21.1 us
    transpose x5, local copies, waits for them, and re-layouts, all_features(): return normed.transpose(1, 0, 2).reshape(rows.shape[0], -1)  15.4 us
    ppermute x6, waiting for transfers between devices, gather_rows(): other = lax.ppermute(held, axis, route)  14.8 us
    reduce_sum x5, other arithmetic, all_features(): mean_square = jnp.mean(values * values, axis=(0, 2), keepdims=True)  10 us
  transfers between devices with their start and end apart: 15, of which 9 were waited for; matrix products, arithmetic and copies ran while one was open for 20% of the time, Pallas kernels for 0%

profile of v1, /device:TPU:0, one launch (start us, length us, event | category | flops | bytes accessed | tf_op | source)
XLA Modules:
  0.0 364.1 jit_solution(9399343363326714552)
XLA Ops:
  7.3 1.7 select_reduce_fusion.11
  11.5 1.7 constant_dynamic-slice_fusion.3
  13.2 3.6 collective-permute-start
  16.9 11.5 %collective-permute-done = bf16[128,2048]{1,0:T(8,128)(2,1)S(1)} collective-permute-done((bf16[128,2048]{1,0:T(8,128)(2,1)S(1)}, bf16[128,2048]{1,0:T(8,128)(2,1)S(1)}, u32[]{:S(2)}, u32[]{:S(2)}) %collective-permute-start) | collective-permute-done | bytes 524320 | tf_op jit(solution)/shard_map/ppermute | solution.py:23
  28.4 1.7 collective-permute-start.7
  30.1 11.0 %collective-permute-done.7 = bf16[128,2048]{1,0:T(8,128)(2,1)S(1)} collective-permute-done((bf16[128,2048]{1,0:T(8,128)(2,1)S(1)}, bf16[128,2048]{1,0:T(8,128)(2,1)S(1)}, u32[]{:S(2)}, u32[]{:S(2)}) %collective-permute-start.7) | collective-permute-done | bytes 524320 | tf_op jit(solution)/shard_map/ppermute | solution.py:23
  41.1 1.4 collective-permute-start.8
  42.6 10.6 %collective-permute-done.8 = bf16[128,2048]{1,0:T(8,128)(2,1)S(1)} collective-permute-done((bf16[128,2048]{1,0:T(8,128)(2,1)S(1)}, bf16[128,2048]{1,0:T(8,128)(2,1)S(1)}, u32[]{:S(2)}, u32[]{:S(2)}) %collective-permute-start.8) | collective-permute-done | bytes 524320 | tf_op jit(solution)/shard_map/ppermute | solution.py:23
  53.2 1.4 collective-permute-start.9
  57.3 6.9 %collective-permute-done.9 = bf16[128,2048]{1,0:T(8,128)(2,1)S(1)} collective-permute-done((bf16[128,2048]{1,0:T(8,128)(2,1)S(1)}, bf16[128,2048]{1,0:T(8,128)(2,1)S(1)}, u32[]{:S(2)}, u32[]{:S(2)}) %collective-permute-start.9) | collective-permute-done | bytes 524320 | tf_op jit(solution)/shard_map/ppermute | solution.py:23
  64.2 3.4 dynamic-slice_select_fusion.3
  77.7 1.8 collective-permute-start.1
  80.3 9.7 %collective-permute-done.1 = bf16[1,2432,128]{2,1,0:T(8,128)(2,1)S(1)} collective-permute-done((bf16[1,2432,128]{2,1,0:T(8,128)(2,1)S(1)}, bf16[1,2432,128]{2,1,0:T(8,128)(2,1)S(1)}, u32[]{:S(2)}, u32[]{:S(2)}) %collective-permute-start.1) | collective-permute-done | bytes 622624 | tf_op jit(solution)/shard_map/ppermute | solution.py:72
  90.1 1.2 maximum_bitcast_fusion
  91.3 2.1 collective-permute-start.2
  94.1 21.1 %copy.114 = bf16[1024,8192]{1,0:T(8,128)(2,1)} copy(bf16[1024,8192]{0,1:T(8,128)(2,1)} %bitcast.405) | data formatting | bytes 33554432 | tf_op jit(solution)/shard_map/dot_general | solution.py:60
  115.9 1.3 iota_compare_fusion.3
  117.2 1.3 iota_compare_fusion.7
  118.5 1.8 iota_compare_fusion.8
  120.3 1.8 iota_compare_fusion.4
  123.0 1.2 multiply_cosine_fusion.7
  124.8 3.6 pad_add_fusion.3
  128.4 1.5 fusion.29
  129.9 2.5 fusion.133
  132.4 1.8 copy.81
  134.2 1.8 reshape.1100
  136.0 2.3 copy.119
  138.4 8.8 %fusion.231 = f32[64,8,128]{2,0,1:T(8,128)S(1)} fusion(bf16[64,8192,1]{1,0,2:T(8,128)(2,1)S(1)} %reshape.1100, bf16[8,128,8192]{2,1,0:T(8,128)(2,1)} %bitcast.391), kind=kOutput, calls=%fused_computation.363 | convolution fusion | flops 1073741824 | bytes 18087936 | tf_op jit(solution)/shard_map/dot_general | solution.py:60
  147.4 2.0 select_bitcast_fusion.1
  153.0 1.4 collective-permute-start.4
  155.3 1.6 collective-permute-done.4
  157.9 3.5 collective-permute-done.5
  163.8 2.2 fusion.17
  166.1 2.1 fusion.11
  168.2 42.3 %all-gather.17.cloned.1.call-done = bf16[512,2048]{1,0:T(8,128)(2,1)} async-done(((bf16[128,2048]{1,0:T(8,128)(2,1)}), bf16[512,2048]{1,0:T(8,128)(2,1)}) %all-gather.17.cloned.1.call-update) | async-done | bytes 2097168 | tf_op jit(solution)/shard_map/all_gather | solution.py:122
  210.5 2.1 fusion.14
  212.5 44.0 %all-gather.13.cloned.1.call-done = bf16[512,2048]{1,0:T(8,128)(2,1)} async-done(((bf16[128,2048]{1,0:T(8,128)(2,1)}), bf16[512,2048]{1,0:T(8,128)(2,1)}) %all-gather.13.cloned.1.call-update) | async-done | bytes 2097168 | tf_op jit(solution)/shard_map/all_gather | solution.py:122
  256.6 2.1 fusion.8
  258.7 6.9 %fusion.89 = (bf16[128,4,2048]{2,0,1:T(8,128)(2,1)S(1)}, bf16[4,16,8,2048]{3,2,1,0:T(8,128)(2,1)S(1)}, bf16[4,16,8,2048]{3,2,1,0:T(8,128)(2,1)S(1)}, bf16[128,4,...) fusion(f32[4,2048]{1,0:T(4,128)S(1)} %copy-done.18, ...), kind=kLoop, calls=%fused_computation.98 | loop fusion | flops 16777216 | bytes 25200640 | tf_op jit(solution)/shard_map/transpose | solution.py:127
  265.7 2.0 copy-done.1
  273.8 3.0 copy.84
  276.7 4.5 %reshape.1088 = bf16[128,8192,1]{1,0,2:T(8,128)(2,1)} reshape(bf16[128,4,2048]{2,1,0:T(4,128)(2,1)} %copy.84) | data formatting | bytes 4194304 | tf_op jit(solution)/shard_map/reshape | solution.py:127
  282.4 3.0 copy.89
  285.4 4.5 %reshape.1091 = bf16[128,8192,1]{1,0,2:T(8,128)(2,1)} reshape(bf16[128,4,2048]{2,1,0:T(4,128)(2,1)} %copy.89) | data formatting | bytes 4194304 | tf_op jit(solution)/shard_map/reshape | solution.py:127
  290.0 4.7 %copy.94 = bf16[128,4,2048]{2,1,0:T(4,128)(2,1)} copy(bf16[128,4,2048]{2,0,1:T(8,128)(2,1)} %get-tuple-element.105) | data formatting | bytes 4194304 | tf_op jit(solution)/shard_map/transpose | solution.py:127
  294.7 4.5 %reshape.1094 = bf16[128,8192,1]{1,0,2:T(8,128)(2,1)} reshape(bf16[128,4,2048]{2,1,0:T(4,128)(2,1)} %copy.94) | data formatting | bytes 4194304 | tf_op jit(solution)/shard_map/reshape | solution.py:127
  301.9 3.0 copy.99
  304.9 3.3 reshape.1097
  308.2 8.3 %fusion.230 = f32[128,8,128]{0,2,1:T(8,128)S(1)} fusion(bf16[128,8192,1]{1,0,2:T(8,128)(2,1)S(1)} %reshape.1097, bf16[8,128,8192]{2,1,0:T(8,128)(2,1)} %bitcast.392), kind=kOutput, calls=%fused_computation.362 | convolution fusion | flops 2147483648 | bytes 19398656 | tf_op jit(solution)/shard_map/dot_general | solution.py:60
  316.6 8.5 %fusion.228 = f32[128,8,128]{0,2,1:T(8,128)S(1)} fusion(bf16[128,8192,1]{1,0,2:T(8,128)(2,1)S(1)} %copy-done.7, bf16[8,128,8192]{2,1,0:T(8,128)(2,1)} %bitcast.393), kind=kOutput, calls=%fused_computation.360 | convolution fusion | flops 2147483648 | bytes 19398656 | tf_op jit(solution)/shard_map/dot_general | solution.py:60
  325.4 4.5 %fusion.226 = f32[128,8,128]{0,2,1:T(8,128)S(1)} fusion(bf16[128,8192,1]{1,0,2:T(8,128)(2,1)S(1)} %copy-done.6, bf16[8,128,8192]{2,1,0:T(8,128)(2,1)S(1)} %bitcast.396), kind=kOutput, calls=%fused_computation.358 | convolution fusion | flops 2147483648 | bytes 19398656 | tf_op jit(solution)/shard_map/dot_general | solution.py:60
  330.0 4.5 %fusion.224 = f32[128,8,128]{0,2,1:T(8,128)S(1)} fusion(bf16[128,8192,1]{1,0,2:T(8,128)(2,1)S(1)} %copy-done.5, bf16[8,128,8192]{2,1,0:T(8,128)(2,1)S(1)} %bitcast.397), kind=kOutput, calls=%fused_computation.356 | convolution fusion | flops 2147483648 | bytes 19398656 | tf_op jit(solution)/shard_map/dot_general | solution.py:60
  335.3 1.1 fusion.5
  336.5 1.5 fusion.1
  338.0 2.2 fusion.61
  340.6 1.9 fusion.7
  342.5 1.5 fusion.3
  344.1 2.0 fusion.49
  346.3 1.1 fusion.4
  347.4 1.5 fusion
  349.0 2.0 fusion.67
  351.2 1.1 fusion.6
  352.3 1.7 fusion.2
  354.1 2.0 fusion.55
  (244 shorter events, 24.9 us)
Async XLA Ops:
  7.2 9.7 %copy-start.33 = (bf16[192,128]{1,0:T(8,128)(2,1)S(1)}, bf16[192,128]{1,0:T(8,128)(2,1)}, u32[]{:S(2)}) copy-start(bf16[192,128]{1,0:T(8,128)(2,1)} %param.19) | copy-start | bytes 147460
  7.2 9.6 %copy-start.34 = (bf16[192,128]{1,0:T(8,128)(2,1)S(1)}, bf16[192,128]{1,0:T(8,128)(2,1)}, u32[]{:S(2)}) copy-start(bf16[192,128]{1,0:T(8,128)(2,1)} %param.18) | copy-start | bytes 147460
  7.2 121.2 %all-gather.11.cloned.1.call-start = ((), (), s32[]{:S(2)}) async-start(), calls=%async_computation | async-start | bytes 1310720 | tf_op jit(solution)/shard_map/all_gather | solution.py:122
  11.5 5.4 %copy-start.19 = (bf16[1024,128]{1,0:T(8,128)(2,1)S(1)}, bf16[1024,128]{1,0:T(8,128)(2,1)}, u32[]{:S(2)}) copy-start(bf16[1024,128]{1,0:T(8,128)(2,1)} %param.17) | copy-start | bytes 786436
  11.5 5.4 %copy-start.20 = (bf16[1024,128]{1,0:T(8,128)(2,1)S(1)}, bf16[1024,128]{1,0:T(8,128)(2,1)}, u32[]{:S(2)}) copy-start(bf16[1024,128]{1,0:T(8,128)(2,1)} %param.16) | copy-start | bytes 786436
  13.2 61.9 %copy-start.51 = (s32[8]{0:T(128)S(1)}, s32[8]{0:T(128)}, u32[]{:S(2)}) copy-start(s32[8]{0:T(128)} %param.22) | copy-start | bytes 100
  13.2 15.2 %collective-permute-start = (bf16[128,2048]{1,0:T(8,128)(2,1)S(1)}, bf16[128,2048]{1,0:T(8,128)(2,1)S(1)}, u32[]{:S(2)}, u32[]{:S(2)}) collective-permute-start(bf16[128,2048]{1,0:T(8,128)(2,1)S(1)} %get-tuple-element.48), channel_id=1, source_target_pairs={{16,0},{20,4},{24,8},{28,12},{0,16},{4,20},{8,24},{12,28},{17,1},{... | collective-permute-start | bytes 1572872 | tf_op jit(solution)/shard_map/ppermute | solution.py:23
  28.4 12.7 %collective-permute-start.7 = (bf16[128,2048]{1,0:T(8,128)(2,1)S(1)}, bf16[128,2048]{1,0:T(8,128)(2,1)S(1)}, u32[]{:S(2)}, u32[]{:S(2)}) collective-permute-start(bf16[128,2048]{1,0:T(8,128)(2,1)S(1)} %get-tuple-element.13), channel_id=1, source_target_pairs={{16,0},{20,4},{24,8},{28,12},{0,16},{4,20},{8,24},{12,28},{17,1},{... | collective-permute-start | bytes 1572872 | tf_op jit(solution)/shard_map/ppermute | solution.py:23
  41.1 12.1 %collective-permute-start.8 = (bf16[128,2048]{1,0:T(8,128)(2,1)S(1)}, bf16[128,2048]{1,0:T(8,128)(2,1)S(1)}, u32[]{:S(2)}, u32[]{:S(2)}) collective-permute-start(bf16[128,2048]{1,0:T(8,128)(2,1)S(1)} %get-tuple-element.15), channel_id=1, source_target_pairs={{16,0},{20,4},{24,8},{28,12},{0,16},{4,20},{8,24},{12,28},{17,1},{... | collective-permute-start | bytes 1572872 | tf_op jit(solution)/shard_map/ppermute | solution.py:23
  42.6 121.2 %all-gather.19.cloned.1.call-start = ((), (), s32[]{:S(2)}) async-start(), calls=%async_computation.4 | async-start | bytes 2621440 | tf_op jit(solution)/shard_map/all_gather | solution.py:122
  53.2 11.0 %collective-permute-start.9 = (bf16[128,2048]{1,0:T(8,128)(2,1)S(1)}, bf16[128,2048]{1,0:T(8,128)(2,1)S(1)}, u32[]{:S(2)}, u32[]{:S(2)}) collective-permute-start(bf16[128,2048]{1,0:T(8,128)(2,1)S(1)} %get-tuple-element.17), channel_id=1, source_target_pairs={{16,0},{20,4},{24,8},{28,12},{0,16},{4,20},{8,24},{12,28},{17,1},{... | collective-permute-start | bytes 1572872 | tf_op jit(solution)/shard_map/ppermute | solution.py:23
  67.6 26.5 %copy-start.35 = (f32[8192]{0:T(1024)S(1)}, f32[8192]{0:T(1024)}, u32[]{:S(2)}) copy-start(f32[8192]{0:T(1024)} %param.14) | copy-start | bytes 98308
  67.6 98.5 %all-gather.15.cloned.1.call-start = ((), (), s32[]{:S(2)}) async-start(), calls=%async_computation.2 | async-start | bytes 2621440 | tf_op jit(solution)/shard_map/all_gather | solution.py:122
  77.7 75.1 %copy-start.49 = (f32[64]{0:T(128)}, f32[64]{0:T(128)S(1)}, u32[]{:S(2)}) copy-start(f32[64]{0:T(128)S(1)} %negate_power_fusion) | copy-start | bytes 772
  77.7 12.3 %collective-permute-start.1 = (bf16[1,2432,128]{2,1,0:T(8,128)(2,1)S(1)}, bf16[1,2432,128]{2,1,0:T(8,128)(2,1)S(1)}, u32[]{:S(2)}, u32[]{:S(2)}) collective-permute-start(bf16[1,2432,128]{2,1,0:T(8,128)(2,1)S(1)} %bitcast.417), channel_id=1, source_target_pairs={{0,16},{4,20},{8,24},{12,28},{16,0},{20,4},{24,8},{28,12},{1,17},{... | collective-permute-start | bytes 1867784 | tf_op jit(solution)/shard_map/ppermute | solution.py:72
  79.5 131.0 %all-gather.17.cloned.1.call-start = ((), (), s32[]{:S(2)}) async-start(), calls=%async_computation.3 | async-start | bytes 2621440 | tf_op jit(solution)/shard_map/all_gather | solution.py:122
  80.2 42.8 %copy-start.52 = (f32[128]{0:T(128)}, f32[128]{0:T(128)S(1)}, u32[]{:S(2)}) copy-start(f32[128]{0:T(128)S(1)} %add_convert_fusion.6) | copy-start | bytes 1540
  80.2 42.7 %copy-start.56 = (f32[128]{0:T(128)}, f32[128]{0:T(128)S(1)}, u32[]{:S(2)}) copy-start(f32[128]{0:T(128)S(1)} %add_convert_fusion.7) | copy-start | bytes 1540
  91.3 33.0 %collective-permute-start.2 = (bf16[2,2432,128]{2,1,0:T(8,128)(2,1)}, bf16[2,2432,128]{2,1,0:T(8,128)(2,1)S(1)}, u32[]{:S(2)}, u32[]{:S(2)}) collective-permute-start(bf16[2,2432,128]{2,1,0:T(8,128)(2,1)} %maximum_bitcast_fusion), channel_id=1, source_target_pairs={{0,8},{4,12},{8,0},{12,4},{16,24},{20,28},{24,16},{28,20},{1,9},{5... | collective-permute-start | bytes 3735560 | tf_op jit(solution)/shard_map/ppermute | solution.py:72
  93.3 29.6 %copy-start.54 = (f32[128]{0:T(128)}, f32[128]{0:T(128)S(1)}, u32[]{:S(2)}) copy-start(f32[128]{0:T(128)S(1)} %add_convert_fusion.8) | copy-start | bytes 1540
  94.1 35.9 %copy-start.17 = (f32[4,2048]{1,0:T(4,128)}, f32[4,2048]{1,0:T(4,128)S(1)}, u32[]{:S(2)}) copy-start(f32[4,2048]{1,0:T(4,128)S(1)} %mul.677) | copy-start | bytes 98308
  115.9 8.8 %copy-start.58 = (f32[128]{0:T(128)}, f32[128]{0:T(128)S(1)}, u32[]{:S(2)}) copy-start(f32[128]{0:T(128)S(1)} %add_convert_fusion.5) | copy-start | bytes 1540
  124.2 132.4 %all-gather.13.cloned.1.call-start = ((), (), s32[]{:S(2)}) async-start(), calls=%async_computation.1 | async-start | bytes 2621440 | tf_op jit(solution)/shard_map/all_gather | solution.py:122
  124.7 22.7 %collective-permute-start.3 = (bf16[4,2432,128]{2,1,0:T(8,128)(2,1)S(1)}, bf16[4,2432,128]{2,1,0:T(8,128)(2,1)}, u32[]{:S(2)}, u32[]{:S(2)}) collective-permute-start(bf16[4,2432,128]{2,1,0:T(8,128)(2,1)S(1)} %bitcast.406), channel_id=1, source_target_pairs={{0,4},{4,0},{8,12},{12,8},{16,20},{20,16},{24,28},{28,24},{1,5},{5... | collective-permute-start | bytes 7471112 | tf_op jit(solution)/shard_map/ppermute | solution.py:72
  138.4 8.8 %copy-start.22 = (f32[64,64]{1,0:T(8,128)S(1)}, f32[64,64]{1,0:T(8,128)}, u32[]{:S(2)}) copy-start(f32[64,64]{1,0:T(8,128)} %get-tuple-element.116) | copy-start | bytes 49156
  138.4 8.8 %copy-start.23 = (f32[64,64]{1,0:T(8,128)S(1)}, f32[64,64]{1,0:T(8,128)}, u32[]{:S(2)}) copy-start(f32[64,64]{1,0:T(8,128)} %get-tuple-element.117) | copy-start | bytes 49156
  151.2 4.1 %copy-start = (bf16[8,1024,256]{2,1,0:T(8,128)(2,1)}, bf16[8,1024,256]{2,1,0:T(8,128)(2,1)S(1)}, u32[]{:S(2)}) copy-start(bf16[8,1024,256]{2,1,0:T(8,128)(2,1)S(1)} %pad_maximum_fusion.1) | copy-start | bytes 12582916
  151.2 3.2 copy-start.32
  153.0 3.9 %collective-permute-start.4 = (bf16[1,2,64,1,128]{4,2,1,3,0:T(8,128)(2,1)S(1)}, bf16[1,2,64,1,128]{4,2,1,3,0:T(8,128)(2,1)S(1)}, u32[]{:S(2)}, u32[]{:S(2)}) collective-permute-start(bf16[1,2,64,1,128]{4,2,1,3,0:T(8,128)(2,1)S(1)} %maximum_bitcast_fusion.22), channel_id=1, source_target_pairs={{0,16},{4,20},{8,24},{12,28},{16,0},{20,4},{24,8},{28,12},{1,17},{... | collective-permute-start | bytes 98312 | tf_op jit(solution)/shard_map/ppermute | solution.py:72
  157.0 4.3 %collective-permute-start.5 = (bf16[2,2,64,1,128]{4,2,1,0,3:T(8,128)(2,1)S(1)}, bf16[2,2,64,1,128]{4,2,1,0,3:T(8,128)(2,1)S(1)}, u32[]{:S(2)}, u32[]{:S(2)}) collective-permute-start(bf16[2,2,64,1,128]{4,2,1,0,3:T(8,128)(2,1)S(1)} %maximum_bitcast_fusion.21), channel_id=1, source_target_pairs={{0,8},{4,12},{8,0},{12,4},{16,24},{20,28},{24,16},{28,20},{1,9},{5... | collective-permute-start | bytes 196616 | tf_op jit(solution)/shard_map/ppermute | solution.py:72
  161.4 1.6 collective-permute-start.6
  163.8 94.9 %copy-start.2 = (bf16[512,2048]{1,0:T(8,128)(2,1)S(1)}, bf16[512,2048]{1,0:T(8,128)(2,1)}, u32[]{:S(2)}) copy-start(bf16[512,2048]{1,0:T(8,128)(2,1)} %all-gather.19.cloned.1.call-done) | copy-start | bytes 6291460
  163.8 94.9 %copy-start.18 = (f32[4,2048]{1,0:T(4,128)S(1)}, f32[4,2048]{1,0:T(4,128)}, u32[]{:S(2)}) copy-start(f32[4,2048]{1,0:T(4,128)} %copy-done.17) | copy-start | bytes 98308
  273.1 8.1 %copy-start.13 = (f32[128,256]{1,0:T(8,128)}, f32[128,256]{1,0:T(8,128)S(1)}, u32[]{:S(2)}) copy-start(f32[128,256]{1,0:T(8,128)S(1)} %fusion.229) | copy-start | bytes 393220
  273.8 7.5 %slice-start.5 = ((f32[128,256]{1,0:T(8,128)}), f32[128,128]{1,0:T(8,128)S(1)}, s32[]{:S(2)}) async-start(f32[128,256]{1,0:T(8,128)} %copy-done.14), calls=%async_computation.10 | async-start | bytes 131072 | tf_op jit(solution)/shard_map/slice | solution.py:160
  273.8 7.6 %slice-start.6 = ((f32[128,256]{1,0:T(8,128)}), f32[128,128]{1,0:T(8,128)S(1)}, s32[]{:S(2)}) async-start(f32[128,256]{1,0:T(8,128)} %copy-done.15), calls=%async_computation.11 | async-start | bytes 131072 | tf_op jit(solution)/shard_map/slice | solution.py:160
  273.8 7.7 %copy-start.50 = (f32[64]{0:T(128)S(1)}, f32[64]{0:T(128)}, u32[]{:S(2)}) copy-start(f32[64]{0:T(128)} %copy-done.49) | copy-start | bytes 772
  273.8 7.7 %copy-start.57 = (f32[128]{0:T(128)S(1)}, f32[128]{0:T(128)}, u32[]{:S(2)}) copy-start(f32[128]{0:T(128)} %copy-done.56) | copy-start | bytes 1540
  273.8 8.6 %copy-start.4 = (bf16[128,4,2048]{2,0,1:T(8,128)(2,1)S(1)}, bf16[128,4,2048]{2,0,1:T(8,128)(2,1)}, u32[]{:S(2)}) copy-start(bf16[128,4,2048]{2,0,1:T(8,128)(2,1)} %get-tuple-element.103) | copy-start | bytes 6291460
  282.4 7.5 %slice-start.7 = ((f32[128,256]{1,0:T(8,128)}), f32[128,128]{1,0:T(8,128)S(1)}, s32[]{:S(2)}) async-start(f32[128,256]{1,0:T(8,128)} %copy-done.16), calls=%async_computation.12 | async-start | bytes 131072 | tf_op jit(solution)/shard_map/slice | solution.py:160
  290.0 9.2 %slice-start.4 = ((f32[128,256]{1,0:T(8,128)}), f32[128,128]{1,0:T(8,128)S(1)}, s32[]{:S(2)}) async-start(f32[128,256]{1,0:T(8,128)} %copy-done.13), calls=%async_computation.9 | async-start | bytes 131072 | tf_op jit(solution)/shard_map/slice | solution.py:160
  290.0 9.3 %copy-start.53 = (f32[128]{0:T(128)S(1)}, f32[128]{0:T(128)}, u32[]{:S(2)}) copy-start(f32[128]{0:T(128)} %copy-done.52) | copy-start | bytes 1540
  290.0 9.3 %copy-start.55 = (f32[128]{0:T(128)S(1)}, f32[128]{0:T(128)}, u32[]{:S(2)}) copy-start(f32[128]{0:T(128)} %copy-done.54) | copy-start | bytes 1540
  290.0 9.3 %copy-start.59 = (f32[128]{0:T(128)S(1)}, f32[128]{0:T(128)}, u32[]{:S(2)}) copy-start(f32[128]{0:T(128)} %copy-done.58) | copy-start | bytes 1540
  290.0 11.9 %copy-start.3 = (bf16[128,4,2048]{2,0,1:T(8,128)(2,1)S(1)}, bf16[128,4,2048]{2,0,1:T(8,128)(2,1)}, u32[]{:S(2)}) copy-start(bf16[128,4,2048]{2,0,1:T(8,128)(2,1)} %get-tuple-element.107) | copy-start | bytes 6291460
  308.2 8.3 %copy-start.7 = (bf16[128,8192,1]{1,0,2:T(8,128)(2,1)S(1)}, bf16[128,8192,1]{1,0,2:T(8,128)(2,1)}, u32[]{:S(2)}) copy-start(bf16[128,8192,1]{1,0,2:T(8,128)(2,1)} %reshape.1094) | copy-start | bytes 6291460
  308.2 16.8 %slice-start = ((s8[16777216]{0:T(1024)(128)(4,1)}), s8[4194304]{0:T(1024)(128)(4,1)S(1)}, s32[]{:S(2)}) async-start(s8[16777216]{0:T(1024)(128)(4,1)} %bitcast.394), calls=%async_computation.5 | async-start | bytes 8388608
  308.2 16.8 %slice-start.1 = ((s8[16777216]{0:T(1024)(128)(4,1)}), s8[4194304]{0:T(1024)(128)(4,1)S(1)}, s32[]{:S(2)}) async-start(s8[16777216]{0:T(1024)(128)(4,1)} %bitcast.394), calls=%async_computation.6 | async-start | bytes 8388608
  316.5 8.5 %slice-start.2 = ((s8[16777216]{0:T(1024)(128)(4,1)}), s8[4194304]{0:T(1024)(128)(4,1)S(1)}, s32[]{:S(2)}) async-start(s8[16777216]{0:T(1024)(128)(4,1)} %bitcast.394), calls=%async_computation.7 | async-start | bytes 8388608
  316.5 8.5 %slice-start.3 = ((s8[16777216]{0:T(1024)(128)(4,1)}), s8[4194304]{0:T(1024)(128)(4,1)S(1)}, s32[]{:S(2)}) async-start(s8[16777216]{0:T(1024)(128)(4,1)} %bitcast.394), calls=%async_computation.8 | async-start | bytes 8388608
  316.5 8.8 %copy-start.6 = (bf16[128,8192,1]{1,0,2:T(8,128)(2,1)S(1)}, bf16[128,8192,1]{1,0,2:T(8,128)(2,1)}, u32[]{:S(2)}) copy-start(bf16[128,8192,1]{1,0,2:T(8,128)(2,1)} %reshape.1091) | copy-start | bytes 6291460
  325.4 4.5 %copy-start.5 = (bf16[128,8192,1]{1,0,2:T(8,128)(2,1)S(1)}, bf16[128,8192,1]{1,0,2:T(8,128)(2,1)}, u32[]{:S(2)}) copy-start(bf16[128,8192,1]{1,0,2:T(8,128)(2,1)} %reshape.1088) | copy-start | bytes 6291460
  329.9 4.6 %copy-start.28 = (f32[128,64]{0,1:T(8,128)S(1)}, f32[128,64]{0,1:T(8,128)}, u32[]{:S(2)}) copy-start(f32[128,64]{0,1:T(8,128)} %get-tuple-element.118) | copy-start | bytes 98308
  329.9 4.6 %copy-start.29 = (f32[128,64]{0,1:T(8,128)S(1)}, f32[128,64]{0,1:T(8,128)}, u32[]{:S(2)}) copy-start(f32[128,64]{0,1:T(8,128)} %get-tuple-element.119) | copy-start | bytes 98308
  329.9 4.6 %copy-start.30 = (f32[128,64]{0,1:T(8,128)S(1)}, f32[128,64]{0,1:T(8,128)}, u32[]{:S(2)}) copy-start(f32[128,64]{0,1:T(8,128)} %get-tuple-element.131) | copy-start | bytes 98308
  329.9 4.6 %copy-start.31 = (f32[128,64]{0,1:T(8,128)S(1)}, f32[128,64]{0,1:T(8,128)}, u32[]{:S(2)}) copy-start(f32[128,64]{0,1:T(8,128)} %get-tuple-element.132) | copy-start | bytes 98308
  329.9 5.4 %copy-start.12 = (pred[128,1728]{0,1:T(8,128)(4,1)S(1)}, pred[128,1728]{0,1:T(8,128)(4,1)}, u32[]{:S(2)}) copy-start(pred[128,1728]{0,1:T(8,128)(4,1)} %get-tuple-element.109) | copy-start | bytes 663556
  329.9 5.4 %copy-start.42 = (bf16[128,1,128]{2,0,1:T(8,128)(2,1)S(1)}, bf16[128,1,128]{2,0,1:T(8,128)(2,1)}, u32[]{:S(2)}) copy-start(bf16[128,1,128]{2,0,1:T(8,128)(2,1)} %copy.91) | copy-start | bytes 98308
  330.0 5.4 %copy-start.48 = (bf16[64,1,128]{2,0,1:T(8,128)(2,1)S(1)}, bf16[64,1,128]{2,0,1:T(8,128)(2,1)}, u32[]{:S(2)}) copy-start(bf16[64,1,128]{2,0,1:T(8,128)(2,1)} %get-tuple-element.82) | copy-start | bytes 49156
  338.0 2.4 copy-start.24
  338.0 2.4 copy-start.25
  338.0 2.4 copy-start.26
  338.0 2.4 copy-start.27
  338.0 2.6 copy-start.11
  (23 other events, 40.4 us)
Sparse Core Ops, SparseCore 0:
  42.7 28.2 all-gather.10
  72.6 45.3 all-gather.18
  119.6 44.6 all-gather.14
  165.8 44.6 all-gather.16
  211.9 44.6 all-gather.12

commit v2 on v1

--- a/solution.py
+++ b/solution.py
@@ -66,15 +66,17 @@
         return lax.all_gather(block, axis, axis=0, tiled=False)
     index = lax.axis_index(axis)
     held = block[None]
-    bit = count // 2
+    places = jnp.zeros((count,), jnp.int32)
+    apart = jnp.arange(count, dtype=jnp.int32) ^ index
+    bit, width = count // 2, 1
     while bit:
-        route = [(i, i ^ bit) for i in range(count)]
-        other = lax.ppermute(held, axis, route)
-        high = (index & bit) != 0
-        held = jnp.stack([jnp.where(high, other, held), jnp.where(high, held, other)], axis=1)
-        held = held.reshape((-1,) + block.shape)
-        bit //= 2
-    return held
+        other = lax.ppermute(held, axis, [(i, i ^ bit) for i in range(count)])
+        held = jnp.concatenate([held, other], axis=0)
+        places = places + jnp.where((apart & bit) != 0, width, 0)
+        bit, width = bit // 2, width * 2
+    return jnp.concatenate(
+        [lax.dynamic_slice_in_dim(held, places[n], 1, axis=0) for n in range(count)], axis=0
+    )
 
 
 def after(value, earlier):
@@ -118,15 +120,17 @@
         start = jnp.clip(slot, 0, slots - 1) * BLK
         return mine, lax.dynamic_slice_in_dim(tokens, start, BLK, axis=0)
 
-    def all_features(rows):
-        gathered = lax.all_gather(rows, "tp", axis=0, tiled=False)
+    def normed_rows(gathered):
         values = gathered.astype(jnp.float32)
         gains = norm_gain.reshape(gathered.shape[0], 1, -1)
         mean_square = jnp.mean(values * values, axis=(0, 2), keepdims=True)
         normed = (values * lax.rsqrt(mean_square + eps_norm) * gains).astype(jnp.bfloat16)
-        return normed.transpose(1, 0, 2).reshape(rows.shape[0], -1)
-
-    full_query = all_features(query_tokens)
+        return normed.transpose(1, 0, 2).reshape(gathered.shape[1], -1)
+
+    def all_features(rows):
+        return lax.all_gather(rows, "tp", axis=0, tiled=False)
+
+    full_query = normed_rows(all_features(query_tokens))
 
     packed = jnp.concatenate([w_key, w_value, cache_key, cache_value], axis=0)
     incoming = []
@@ -188,7 +192,13 @@
         length = of_position(position, seg_lengths)
         owner = of_position(position, prompt_query)
         offset = lax.dynamic_index_in_dim(query_lengths, owner, 0, keepdims=False)
-        queries, keys, values = project(all_features(blocks[c]), INSTR + offset + passage_rows)
+        rows = blocks[c]
+        if c >= 2:
+            rows, block_out[c - 2] = after(rows, block_out[c - 2])
+        gathered = all_features(rows)
+        if c:
+            gathered, block_out[c - 1] = after(gathered, block_out[c - 1])
+        queries, keys, values = project(normed_rows(gathered), INSTR + offset + passage_rows)
         text = lax.dynamic_slice(
             text_all,
             (owner // local_queries, 0, owner % local_queries, 0, 0, 0),

time: 370 us -> 361 us (0.976)
  waiting for transfers between devices: 141 us -> 97 us
  matrix products: 53.3 us -> 70.6 us
  between operations: 30.8 us -> 46 us
  other arithmetic: 51.6 us -> 59 us
  local copies, waits for them, and re-layouts: 73.1 us -> 69.1 us
    ppermute x4, waiting for transfers between devices: 40 us -> 20.4 us  [passed_along(): return lax.ppermute(block, axis, route)]
    all_gather x5, waiting for transfers between devices: 86.3 us -> 69.8 us  [all_features(): return lax.all_gather(rows, 'tp', axis=0, tiled=False)]
    dot_general x10, matrix products: 38.1 us -> 51.8 us  [matmul(): return jnp.dot(left, right, preferred_element_type=jnp.float32)]
    ppermute x6, waiting for transfers between devices: 14.8 us -> 6.15 us  [gather_rows(): other = lax.ppermute(held, axis, [(i, i ^ bit) for i in range(count)])]
    concatenate x0 -> x6, other arithmetic: none -> 5.93 us  [gather_rows(): held = jnp.concatenate([held, other], axis=0)]
    transpose x2 -> x5, other arithmetic: 9.38 us -> 12.4 us  [normed_rows(): return normed.transpose(1, 0, 2).reshape(gathered.shape[1], -1)]
  transfers between devices with their start and end apart: 15 -> 15, of which waited for: 9 -> 7; matrix products, arithmetic and copies ran while one was open for 20% -> 36% of each run, Pallas kernels for 0% -> 0%
where the time goes in v2:
time: 361 us; the launch traced here: 356 us
  waiting for transfers between devices  97 us (27%)
  matrix products  70.6 us (20%)
  local copies, waits for them, and re-layouts  69.1 us (19%)
  other arithmetic  59 us (16%)
  between operations  46 us (13%)
  starting transfers between devices  14 us (4%)
    all_gather x5, waiting for transfers between devices, all_features(): return lax.all_gather(rows, 'tp', axis=0, tiled=False)  69.8 us
    dot_general x10, matrix products, matmul(): return jnp.dot(left, right, preferred_element_type=jnp.float32)  51.8 us
    reshape x10, local copies, waits for them, and re-layouts, normed_rows(): return normed.transpose(1, 0, 2).reshape(gathered.shape[1], -1)  21.6 us
    dot_general x1, local copies, waits for them, and re-layouts, matmul(): return jnp.dot(left, right, preferred_element_type=jnp.float32)  21.4 us
    ppermute x4, waiting for transfers between devices, passed_along(): return lax.ppermute(block, axis, route)  20.4 us
    transpose x5, local copies, waits for them, and re-layouts, normed_rows(): return normed.transpose(1, 0, 2).reshape(gathered.shape[1], -1)  14.1 us
    transpose x5, other arithmetic, normed_rows(): return normed.transpose(1, 0, 2).reshape(gathered.shape[1], -1)  12.4 us
    dot_general x5, matrix products, attend(): jnp.einsum('hgrk,khd->rhgd', weights, values_all, preferred_element_type=...  10.2 us
  transfers between devices with their start and end apart: 15, of which 7 were waited for; matrix products, arithmetic and copies ran while one was open for 36% of the time, Pallas kernels for 0%

profile of v2, /device:TPU:0, one launch (start us, length us, event | category | flops | bytes accessed | tf_op | source)
XLA Modules:
  0.0 355.6 jit_solution(16756867811986546176)
XLA Ops:
  8.0 1.6 select_reduce_fusion.1
  11.5 1.5 constant_dynamic-slice_fusion
  13.0 3.4 collective-permute-start
  17.6 10.8 %collective-permute-done = bf16[128,2048]{1,0:T(8,128)(2,1)S(1)} collective-permute-done((bf16[128,2048]{1,0:T(8,128)(2,1)S(1)}, bf16[128,2048]{1,0:T(8,128)(2,1)S(1)}, u32[]{:S(2)}, u32[]{:S(2)}) %collective-permute-start) | collective-permute-done | bytes 524320 | tf_op jit(solution)/shard_map/ppermute | solution.py:23
  28.4 1.7 collective-permute-start.1
  32.0 9.6 %collective-permute-done.1 = bf16[128,2048]{1,0:T(8,128)(2,1)S(1)} collective-permute-done((bf16[128,2048]{1,0:T(8,128)(2,1)S(1)}, bf16[128,2048]{1,0:T(8,128)(2,1)S(1)}, u32[]{:S(2)}, u32[]{:S(2)}) %collective-permute-start.1) | collective-permute-done | bytes 524320 | tf_op jit(solution)/shard_map/ppermute | solution.py:23
  41.6 2.7 dynamic-slice_select_fusion.1
  56.1 1.2 iota_compare_fusion.7
  57.3 1.3 iota_compare_fusion.3
  60.8 1.8 collective-permute-start.3
  62.6 3.4 pad_add_fusion
  66.2 1.8 iota_compare_fusion.8
  80.1 21.4 %copy.82 = bf16[1024,8192]{1,0:T(8,128)(2,1)} copy(bf16[1024,8192]{0,1:T(8,128)(2,1)} %bitcast.352) | data formatting | bytes 33554432 | tf_op jit(solution)/shard_map/dot_general | solution.py:60
  106.6 1.8 iota_compare_fusion.4
  110.2 1.4 collective-permute-start.4
  111.6 1.5 collective-permute-start.9
  113.1 1.5 fusion.29
  114.6 2.5 fusion.133
  117.2 1.8 copy.51
  118.9 2.6 reshape.1086
  121.5 9.1 %fusion.234 = f32[64,8,128]{2,0,1:T(8,128)S(1)} fusion(bf16[64,8192,1]{1,0,2:T(8,128)(2,1)} %reshape.1086, bf16[8,128,8192]{2,1,0:T(8,128)(2,1)} %bitcast.342), kind=kOutput, calls=%fused_computation.373 | convolution fusion | flops 1073741824 | bytes 18087936 | tf_op jit(solution)/shard_map/dot_general | solution.py:60
  132.5 2.7 dynamic-slice_select_fusion.3
  135.3 2.4 collective-permute-done.4
  137.7 1.8 pad_maximum_fusion.2
  139.5 2.1 fusion.17
  141.7 2.4 fusion.83
  144.4 3.0 copy.52
  147.3 4.5 %reshape.1074 = bf16[128,8192,1]{1,0,2:T(8,128)(2,1)} reshape(bf16[128,4,2048]{2,1,0:T(4,128)(2,1)} %copy.52) | data formatting | bytes 4194304 | tf_op jit(solution)/shard_map/reshape | solution.py:128
  151.8 8.8 %fusion.227 = f32[128,8,128]{0,2,1:T(8,128)S(1)} fusion(bf16[128,8192,1]{1,0,2:T(8,128)(2,1)} %reshape.1074, bf16[8,128,8192]{2,1,0:T(8,128)(2,1)} %bitcast.343), kind=kOutput, calls=%fused_computation.366 | convolution fusion | flops 2147483648 | bytes 19398656 | tf_op jit(solution)/shard_map/dot_general | solution.py:60
  161.4 2.9 pad_maximum_fusion
  169.3 1.3 collective-permute-start.6
  171.5 1.9 fusion.224
  175.9 1.8 collective-permute-start.7
  177.8 2.4 collective-permute-done.7
  180.3 1.3 collective-permute-done.8
  183.6 1.5 fusion
  185.1 2.7 fusion.67
  187.9 2.1 fusion.8
  190.0 2.4 fusion.89
  192.6 3.4 copy.57
  196.0 4.5 %reshape.1077 = bf16[128,8192,1]{1,0,2:T(8,128)(2,1)} reshape(bf16[128,4,2048]{2,1,0:T(4,128)(2,1)} %copy.57) | data formatting | bytes 4194304 | tf_op jit(solution)/shard_map/reshape | solution.py:128
  200.5 8.7 %fusion.229 = f32[128,8,128]{0,2,1:T(8,128)S(1)} fusion(bf16[128,8192,1]{1,0,2:T(8,128)(2,1)} %reshape.1077, bf16[8,128,8192]{2,1,0:T(8,128)(2,1)} %bitcast.344), kind=kOutput, calls=%fused_computation.368 | convolution fusion | flops 2147483648 | bytes 19398656 | tf_op jit(solution)/shard_map/dot_general | solution.py:60
  209.4 3.0 fusion.228
  214.0 2.1 fusion.5
  216.2 1.5 fusion.1
  217.7 2.7 fusion.61
  220.4 35.4 %all-gather.17.cloned.1.call-done = bf16[512,2048]{1,0:T(8,128)(2,1)} async-done(((bf16[128,2048]{1,0:T(8,128)(2,1)}), bf16[512,2048]{1,0:T(8,128)(2,1)}) %all-gather.17.cloned.1.call-update) | async-done | bytes 2097168 | tf_op jit(solution)/shard_map/all_gather | solution.py:131
  255.8 2.1 fusion.11
  257.9 2.4 fusion.87
  260.6 3.0 copy.62
  263.6 4.6 %reshape.1080 = bf16[128,8192,1]{1,0,2:T(8,128)(2,1)} reshape(bf16[128,4,2048]{2,1,0:T(4,128)(2,1)} %copy.62) | data formatting | bytes 4194304 | tf_op jit(solution)/shard_map/reshape | solution.py:128
  268.2 8.7 %fusion.231 = f32[128,8,128]{0,2,1:T(8,128)S(1)} fusion(bf16[128,8192,1]{1,0,2:T(8,128)(2,1)} %reshape.1080, bf16[8,128,8192]{2,1,0:T(8,128)(2,1)} %bitcast.345), kind=kOutput, calls=%fused_computation.370 | convolution fusion | flops 2147483648 | bytes 19398656 | tf_op jit(solution)/shard_map/dot_general | solution.py:60
  277.0 2.9 fusion.230
  281.6 2.3 fusion.6
  283.9 1.4 fusion.2
  285.4 2.0 fusion.55
  287.5 34.4 %all-gather.19.cloned.1.call-done = bf16[512,2048]{1,0:T(8,128)(2,1)} async-done(((bf16[128,2048]{1,0:T(8,128)(2,1)}), bf16[512,2048]{1,0:T(8,128)(2,1)}) %all-gather.19.cloned.1.call-update) | async-done | bytes 2097168 | tf_op jit(solution)/shard_map/all_gather | solution.py:131
  321.8 2.1 fusion.14
  323.9 2.6 fusion.85
  328.0 3.0 copy.67
  331.0 3.5 reshape.1083
  334.5 8.2 %fusion.233 = f32[128,8,128]{0,2,1:T(8,128)S(1)} fusion(bf16[128,8192,1]{1,0,2:T(8,128)(2,1)S(1)} %reshape.1083, bf16[8,128,8192]{2,1,0:T(8,128)(2,1)} %bitcast.346), kind=kOutput, calls=%fused_computation.372 | convolution fusion | flops 2147483648 | bytes 19398656 | tf_op jit(solution)/shard_map/dot_general | solution.py:60
  344.0 1.5 fusion.3
  345.5 2.0 fusion.49
  (211 shorter events, 29.2 us)
Async XLA Ops:
  7.2 105.9 %all-gather.13.cloned.1.call-start = ((), (), s32[]{:S(2)}) async-start(), calls=%async_computation.1 | async-start | bytes 1310720 | tf_op jit(solution)/shard_map/all_gather | solution.py:131
  7.9 131.6 %all-gather.15.cloned.1.call-start = ((), (), s32[]{:S(2)}) async-start(), calls=%async_computation.2 | async-start | bytes 2621440 | tf_op jit(solution)/shard_map/all_gather | solution.py:131
  11.5 40.7 %copy-start.35 = (s32[8]{0:T(128)S(1)}, s32[8]{0:T(128)}, u32[]{:S(2)}) copy-start(s32[8]{0:T(128)} %param.22) | copy-start | bytes 100
  13.0 66.4 %copy-start.27 = (f32[8192]{0:T(1024)S(1)}, f32[8192]{0:T(1024)}, u32[]{:S(2)}) copy-start(f32[8192]{0:T(1024)} %param.14) | copy-start | bytes 98308
  13.0 15.4 %collective-permute-start = (bf16[128,2048]{1,0:T(8,128)(2,1)S(1)}, bf16[128,2048]{1,0:T(8,128)(2,1)S(1)}, u32[]{:S(2)}, u32[]{:S(2)}) collective-permute-start(bf16[128,2048]{1,0:T(8,128)(2,1)S(1)} %get-tuple-element.67), channel_id=1, source_target_pairs={{16,0},{20,4},{24,8},{28,12},{0,16},{4,20},{8,24},{12,28},{17,1},{... | collective-permute-start | bytes 1572872 | tf_op jit(solution)/shard_map/ppermute | solution.py:23
  28.4 13.2 %collective-permute-start.1 = (bf16[128,2048]{1,0:T(8,128)(2,1)S(1)}, bf16[128,2048]{1,0:T(8,128)(2,1)S(1)}, u32[]{:S(2)}, u32[]{:S(2)}) collective-permute-start(bf16[128,2048]{1,0:T(8,128)(2,1)S(1)} %get-tuple-element.21), channel_id=1, source_target_pairs={{16,0},{20,4},{24,8},{28,12},{0,16},{4,20},{8,24},{12,28},{17,1},{... | collective-permute-start | bytes 1572872 | tf_op jit(solution)/shard_map/ppermute | solution.py:23
  44.3 143.6 %all-gather.11.cloned.1.call-start = ((), (), s32[]{:S(2)}) async-start(), calls=%async_computation | async-start | bytes 2621440 | tf_op jit(solution)/shard_map/all_gather | solution.py:131
  55.4 46.1 %copy-start.38 = (f32[64]{0:T(128)}, f32[64]{0:T(128)S(1)}, u32[]{:S(2)}) copy-start(f32[64]{0:T(128)S(1)} %add_convert_fusion.9) | copy-start | bytes 772
  56.1 45.4 %copy-start.40 = (pred[64]{0:T(512)(128)(4,1)}, pred[64]{0:T(512)(128)(4,1)S(1)}, u32[]{:S(2)}) copy-start(pred[64]{0:T(512)(128)(4,1)S(1)} %iota_compare_fusion.2) | copy-start | bytes 196
  58.6 42.9 %copy-start.36 = (f32[128]{0:T(128)}, f32[128]{0:T(128)S(1)}, u32[]{:S(2)}) copy-start(f32[128]{0:T(128)S(1)} %get-tuple-element.168) | copy-start | bytes 1540
  60.8 48.2 %collective-permute-start.3 = (bf16[1,2432,128]{2,1,0:T(8,128)(2,1)S(1)}, bf16[1,2432,128]{2,1,0:T(8,128)(2,1)S(1)}, u32[]{:S(2)}, u32[]{:S(2)}) collective-permute-start(bf16[1,2432,128]{2,1,0:T(8,128)(2,1)S(1)} %bitcast.353), channel_id=1, source_target_pairs={{0,16},{4,20},{8,24},{12,28},{16,0},{20,4},{24,8},{28,12},{1,17},{... | collective-permute-start | bytes 1867784 | tf_op jit(solution)/shard_map/ppermute | solution.py:73
  66.0 45.6 %collective-permute-start.2 = (bf16[128,2048]{1,0:T(8,128)(2,1)S(1)}, bf16[128,2048]{1,0:T(8,128)(2,1)}, u32[]{:S(2)}, u32[]{:S(2)}) collective-permute-start(bf16[128,2048]{1,0:T(8,128)(2,1)S(1)} %get-tuple-element.22), channel_id=1, source_target_pairs={{16,0},{20,4},{24,8},{28,12},{0,16},{4,20},{8,24},{12,28},{17,1},{... | collective-permute-start | bytes 1572872 | tf_op jit(solution)/shard_map/ppermute | solution.py:23
  108.4 147.4 %all-gather.17.cloned.1.call-start = ((), (), s32[]{:S(2)}) async-start(), calls=%async_computation.3 | async-start | bytes 2621440 | tf_op jit(solution)/shard_map/all_gather | solution.py:131
  110.2 27.5 %collective-permute-start.4 = (bf16[2,2432,128]{2,1,0:T(8,128)(2,1)}, bf16[2,2432,128]{2,1,0:T(8,128)(2,1)S(1)}, u32[]{:S(2)}, u32[]{:S(2)}) collective-permute-start(bf16[2,2432,128]{2,1,0:T(8,128)(2,1)} %pad_maximum_fusion.3), channel_id=1, source_target_pairs={{0,8},{4,12},{8,0},{12,4},{16,24},{20,28},{24,16},{28,20},{1,9},{5... | collective-permute-start | bytes 3735560 | tf_op jit(solution)/shard_map/ppermute | solution.py:73
  111.6 21.0 %collective-permute-start.9 = (bf16[128,2048]{1,0:T(8,128)(2,1)}, bf16[128,2048]{1,0:T(8,128)(2,1)S(1)}, u32[]{:S(2)}, u32[]{:S(2)}) collective-permute-start(bf16[128,2048]{1,0:T(8,128)(2,1)} %get-tuple-element.29), channel_id=1, source_target_pairs={{16,0},{20,4},{24,8},{28,12},{0,16},{4,20},{8,24},{12,28},{17,1},{... | collective-permute-start | bytes 1572872 | tf_op jit(solution)/shard_map/ppermute | solution.py:23
  121.5 9.1 %copy-start.4 = (bf16[4,8,8,2048]{3,2,1,0:T(8,128)(2,1)S(1)}, bf16[4,8,8,2048]{3,2,1,0:T(8,128)(2,1)}, u32[]{:S(2)}) copy-start(bf16[4,8,8,2048]{3,2,1,0:T(8,128)(2,1)} %get-tuple-element.79) | copy-start | bytes 3145732
  137.7 6.4 %copy-start.2 = (bf16[2,2432,128]{2,1,0:T(8,128)(2,1)}, bf16[2,2432,128]{2,1,0:T(8,128)(2,1)S(1)}, u32[]{:S(2)}) copy-start(bf16[2,2432,128]{2,1,0:T(8,128)(2,1)S(1)} %collective-permute-done.4) | copy-start | bytes 3735556
  139.5 21.9 %collective-permute-start.5 = (bf16[4,2432,128]{2,1,0:T(8,128)(2,1)}, bf16[4,2432,128]{2,1,0:T(8,128)(2,1)}, u32[]{:S(2)}, u32[]{:S(2)}) collective-permute-start(bf16[4,2432,128]{2,1,0:T(8,128)(2,1)} %pad_maximum_fusion.2), channel_id=1, source_target_pairs={{0,4},{4,0},{8,12},{12,8},{16,20},{20,16},{24,28},{28,24},{1,5},{5... | collective-permute-start | bytes 7471112 | tf_op jit(solution)/shard_map/ppermute | solution.py:73
  151.8 8.8 %copy-start.24 = (f32[128,64]{0,1:T(8,128)S(1)}, f32[128,64]{0,1:T(8,128)}, u32[]{:S(2)}) copy-start(f32[128,64]{0,1:T(8,128)} %get-tuple-element.137) | copy-start | bytes 98308
  151.8 8.9 %copy-start.25 = (f32[128,64]{0,1:T(8,128)S(1)}, f32[128,64]{0,1:T(8,128)}, u32[]{:S(2)}) copy-start(f32[128,64]{0,1:T(8,128)} %get-tuple-element.138) | copy-start | bytes 98308
  151.8 9.6 %copy-start.3 = (bf16[2,2432,128]{2,1,0:T(8,128)(2,1)S(1)}, bf16[2,2432,128]{2,1,0:T(8,128)(2,1)}, u32[]{:S(2)}) copy-start(bf16[2,2432,128]{2,1,0:T(8,128)(2,1)} %copy-done.2) | copy-start | bytes 3735556
  166.2 18.9 %copy-start.10 = (bf16[8,192,128]{2,1,0:T(8,128)(2,1)}, bf16[8,192,128]{2,1,0:T(8,128)(2,1)S(1)}, u32[]{:S(2)}) copy-start(bf16[8,192,128]{2,1,0:T(8,128)(2,1)S(1)} %get-tuple-element.58) | copy-start | bytes 1179652
  166.2 1.4 copy-start.5
  166.7 4.7 %copy-start = (bf16[8,1024,256]{2,1,0:T(8,128)(2,1)}, bf16[8,1024,256]{2,1,0:T(8,128)(2,1)S(1)}, u32[]{:S(2)}) copy-start(bf16[8,1024,256]{2,1,0:T(8,128)(2,1)S(1)} %pad_maximum_fusion.1) | copy-start | bytes 12582916
  166.7 2.3 copy-start.39
  168.3 3.2 copy-start.17
  168.4 3.2 copy-start.18
  168.4 3.2 copy-start.26
  169.3 6.6 %collective-permute-start.6 = (bf16[1,2,64,1,128]{4,2,1,3,0:T(8,128)(2,1)S(1)}, bf16[1,2,64,1,128]{4,2,1,3,0:T(8,128)(2,1)S(1)}, u32[]{:S(2)}, u32[]{:S(2)}) collective-permute-start(bf16[1,2,64,1,128]{4,2,1,3,0:T(8,128)(2,1)S(1)} %maximum_bitcast_fusion.20), channel_id=1, source_target_pairs={{0,16},{4,20},{8,24},{12,28},{16,0},{20,4},{24,8},{28,12},{1,17},{... | collective-permute-start | bytes 98312 | tf_op jit(solution)/shard_map/ppermute | solution.py:73
  171.4 2.7 copy-start.34
  171.4 2.7 copy-start.41
  174.1 0.8 copy-start.37
  174.1 8.4 %copy-start.9 = (pred[128,1728]{0,1:T(8,128)(4,1)S(1)}, pred[128,1728]{0,1:T(8,128)(4,1)}, u32[]{:S(2)}) copy-start(pred[128,1728]{0,1:T(8,128)(4,1)} %get-tuple-element.113) | copy-start | bytes 663556
  174.1 8.4 %copy-start.14 = (bf16[8,192,128]{2,1,0:T(8,128)(2,1)S(1)}, bf16[8,192,128]{2,1,0:T(8,128)(2,1)}, u32[]{:S(2)}) copy-start(bf16[8,192,128]{2,1,0:T(8,128)(2,1)} %get-tuple-element.59) | copy-start | bytes 1179652
  174.1 8.4 %copy-start.16 = (bf16[128,8,64]{0,2,1:T(8,128)(2,1)S(1)}, bf16[128,8,64]{0,2,1:T(8,128)(2,1)}, u32[]{:S(2)}) copy-start(bf16[128,8,64]{0,2,1:T(8,128)(2,1)} %get-tuple-element.87) | copy-start | bytes 393220
  175.9 4.3 %collective-permute-start.7 = (bf16[2,2,64,1,128]{4,2,1,3,0:T(8,128)(2,1)S(1)}, bf16[2,2,64,1,128]{4,2,1,3,0:T(8,128)(2,1)S(1)}, u32[]{:S(2)}, u32[]{:S(2)}) collective-permute-start(bf16[2,2,64,1,128]{4,2,1,3,0:T(8,128)(2,1)S(1)} %pad_maximum_fusion.8), channel_id=1, source_target_pairs={{0,8},{4,12},{8,0},{12,4},{16,24},{20,28},{24,16},{28,20},{1,9},{5... | collective-permute-start | bytes 196616 | tf_op jit(solution)/shard_map/ppermute | solution.py:73
  180.2 1.4 collective-permute-start.8
  183.6 1.5 copy-start.45
  209.3 4.6 %copy-start.22 = (f32[128,64]{0,1:T(8,128)S(1)}, f32[128,64]{0,1:T(8,128)}, u32[]{:S(2)}) copy-start(f32[128,64]{0,1:T(8,128)} %get-tuple-element.133) | copy-start | bytes 98308
  209.3 4.6 %copy-start.23 = (f32[128,64]{0,1:T(8,128)S(1)}, f32[128,64]{0,1:T(8,128)}, u32[]{:S(2)}) copy-start(f32[128,64]{0,1:T(8,128)} %get-tuple-element.134) | copy-start | bytes 98308
  209.3 4.7 %copy-start.8 = (pred[128,1728]{0,1:T(8,128)(4,1)S(1)}, pred[128,1728]{0,1:T(8,128)(4,1)}, u32[]{:S(2)}) copy-start(pred[128,1728]{0,1:T(8,128)(4,1)} %get-tuple-element.111) | copy-start | bytes 663556
  209.3 4.7 %copy-start.33 = (bf16[64,1,128]{2,0,1:T(8,128)(2,1)S(1)}, bf16[64,1,128]{2,0,1:T(8,128)(2,1)}, u32[]{:S(2)}) copy-start(bf16[64,1,128]{2,0,1:T(8,128)(2,1)} %get-tuple-element.96) | copy-start | bytes 49156
  209.3 112.5 %all-gather.19.cloned.1.call-start = ((), (), s32[]{:S(2)}) async-start(), calls=%async_computation.4 | async-start | bytes 2621440 | tf_op jit(solution)/shard_map/all_gather | solution.py:131
  216.2 1.5 copy-start.11
  216.2 1.5 copy-start.32
  216.2 1.5 copy-start.43
  277.0 4.5 %copy-start.20 = (f32[128,64]{0,1:T(8,128)S(1)}, f32[128,64]{0,1:T(8,128)}, u32[]{:S(2)}) copy-start(f32[128,64]{0,1:T(8,128)} %get-tuple-element.135) | copy-start | bytes 98308
  277.0 4.5 %copy-start.21 = (f32[128,64]{0,1:T(8,128)S(1)}, f32[128,64]{0,1:T(8,128)}, u32[]{:S(2)}) copy-start(f32[128,64]{0,1:T(8,128)} %get-tuple-element.136) | copy-start | bytes 98308
  277.0 4.6 %copy-start.31 = (bf16[64,1,128]{2,0,1:T(8,128)(2,1)S(1)}, bf16[64,1,128]{2,0,1:T(8,128)(2,1)}, u32[]{:S(2)}) copy-start(bf16[64,1,128]{2,0,1:T(8,128)(2,1)} %get-tuple-element.95) | copy-start | bytes 49156
  281.6 2.3 copy-start.7
  283.9 1.5 copy-start.12
  283.9 1.5 copy-start.30
  283.9 1.5 copy-start.44
  323.9 2.8 copy-start.1
  334.4 8.3 %copy-start.19 = (f32[128,64]{0,1:T(8,128)S(1)}, f32[128,64]{0,1:T(8,128)}, u32[]{:S(2)}) copy-start(f32[128,64]{0,1:T(8,128)} %get-tuple-element.121) | copy-start | bytes 98308
  334.4 8.3 %copy-start.6 = (pred[128,1728]{0,1:T(8,128)(4,1)S(1)}, pred[128,1728]{0,1:T(8,128)(4,1)}, u32[]{:S(2)}) copy-start(pred[128,1728]{0,1:T(8,128)(4,1)} %get-tuple-element.110) | copy-start | bytes 663556
  334.4 8.3 %copy-start.15 = (bf16[8,192,128]{2,1,0:T(8,128)(2,1)S(1)}, bf16[8,192,128]{2,1,0:T(8,128)(2,1)}, u32[]{:S(2)}) copy-start(bf16[8,192,128]{2,1,0:T(8,128)(2,1)} %get-tuple-element.59) | copy-start | bytes 1179652
  334.5 8.3 %copy-start.29 = (bf16[64,1,128]{2,0,1:T(8,128)(2,1)S(1)}, bf16[64,1,128]{2,0,1:T(8,128)(2,1)}, u32[]{:S(2)}) copy-start(bf16[64,1,128]{2,0,1:T(8,128)(2,1)} %get-tuple-element.94) | copy-start | bytes 49156
  343.9 1.5 copy-start.13
  344.0 1.5 copy-start.28
  344.0 1.5 copy-start.42
Sparse Core Ops, SparseCore 0:
  9.6 30.6 all-gather.12
  44.4 47.1 all-gather.14
  108.6 47.0 all-gather.10
  209.4 46.3 all-gather.16
  277.1 44.6 all-gather.18
